TPU v7x, 512 devices: a whole 4x4x16 slice. The times are simulated.
512 devices in a mesh: rep: 16 (over z_hi, y), fsdp: 8 (over z_lo, core), tp: 4 (over x).
Axes of the slice: x: 4, y: 4, z: 16 (z_hi: 4, z_lo: 4; z = z_hi * 4 + z_lo), core: 2. Of those that a mesh axis runs over, the one named last changes fastest.
Arguments:
- partner: int32 [3, 16], replicated, may hold values from 0 to 15, as said below
- weight_gate: float32 [16, 128, 25600], P('rep', 'fsdp', 'tp'), may hold values from -6 to 6
- weight_up: float32 [16, 128, 25600], P('rep', 'fsdp', 'tp'), may hold values from -6 to 6
- weight_down: float32 [16, 128, 5120], P('rep', 'fsdp', 'tp'), may hold values from -6 to 6
- moment_gate: float32 [16, 128, 25600], P('rep', 'fsdp', 'tp'), may hold values from -6 to 6
- moment_up: float32 [16, 128, 25600], P('rep', 'fsdp', 'tp'), may hold values from -6 to 6
- moment_down: float32 [16, 128, 5120], P('rep', 'fsdp', 'tp'), may hold values from -6 to 6
- grad_gate: bfloat16 [16, 128, 25600], P('rep', 'fsdp', 'tp')
- grad_up: bfloat16 [16, 128, 25600], P('rep', 'fsdp', 'tp')
- grad_down: bfloat16 [16, 128, 5120], P('rep', 'fsdp', 'tp')
Outputs:
- new_weight_gate: float32 [16, 128, 25600], P('rep', 'fsdp', 'tp')
- new_weight_up: float32 [16, 128, 25600], P('rep', 'fsdp', 'tp')
- new_weight_down: float32 [16, 128, 5120], P('rep', 'fsdp', 'tp')
- new_moment_gate: float32 [16, 128, 25600], P('rep', 'fsdp', 'tp')
- new_moment_up: float32 [16, 128, 25600], P('rep', 'fsdp', 'tp')
- new_moment_down: float32 [16, 128, 5120], P('rep', 'fsdp', 'tp')
Inputs may be any that keep to these rules, and one draw needn't show every extreme that they name: Each row of partner is a matching: partner[m, partner[m, r]] = r and partner[m, r] != r for every replica r.
All inputs are finite; a program needn't handle non-finite values.
Results may differ from a plain program's by a relative error of at most 0.0003.
Values may be sent and summed in bfloat16 or wider, within the bound.
No kernel may reach another device: no remote copies, remote signals or barrier semaphores. Data moves between devices by JAX's collectives and lax.ppermute only.
A program may use at most 64 MiB of HBM per device.

v0:
```python
import jax
import jax.numpy as jnp
from jax import lax
from jax.sharding import PartitionSpec as P

CLIP_RATIO = 0.5
BETA = 0.9
GAMMA = 0.4
RATE = 0.7
EPS = 1e-06


def home_norm(mixed_all):
    partials = jnp.stack([jnp.sum(jnp.square(mixed)) for mixed in mixed_all])
    return lax.psum(partials, ("fsdp", "tp"))


def local(
    partner,
    weight_gate,
    weight_up,
    weight_down,
    moment_gate,
    moment_up,
    moment_down,
    grad_gate,
    grad_up,
    grad_down,
):
    weights = (weight_gate, weight_up, weight_down)
    moments = (moment_gate, moment_up, moment_down)
    grads = (grad_gate, grad_up, grad_down)
    middle_totals = None
    spread_weights = (
        lax.all_to_all(weight_gate, "rep", split_axis=1, concat_axis=0, tiled=True),
        lax.all_to_all(weight_up, "rep", split_axis=1, concat_axis=0, tiled=True),
        lax.all_to_all(weight_down, "rep", split_axis=1, concat_axis=0, tiled=True),
    )
    spread_grads = (
        lax.all_to_all(grad_gate, "rep", split_axis=1, concat_axis=0, tiled=True),
        lax.all_to_all(grad_up, "rep", split_axis=1, concat_axis=0, tiled=True),
        lax.all_to_all(grad_down, "rep", split_axis=1, concat_axis=0, tiled=True),
    )
    paired_weights = tuple(
        (jnp.take(spread_weights[slot], partner[slot], axis=0) for slot in range(3))
    )
    paired_grads = tuple((jnp.take(spread_grads[slot], partner[slot], axis=0) for slot in range(3)))
    mate_weights = (
        lax.all_to_all(paired_weights[0], "rep", split_axis=0, concat_axis=1, tiled=True),
        lax.all_to_all(paired_weights[1], "rep", split_axis=0, concat_axis=1, tiled=True),
        lax.all_to_all(paired_weights[2], "rep", split_axis=0, concat_axis=1, tiled=True),
    )
    mate_grads = (
        lax.all_to_all(paired_grads[0], "rep", split_axis=0, concat_axis=1, tiled=True),
        lax.all_to_all(paired_grads[1], "rep", split_axis=0, concat_axis=1, tiled=True),
        lax.all_to_all(paired_grads[2], "rep", split_axis=0, concat_axis=1, tiled=True),
    )
    mixed_all = tuple(
        (0.5 * (g.astype(jnp.float32) + h.astype(jnp.float32)) for g, h in zip(grads, mate_grads))
    )
    totals = home_norm(mixed_all)
    results_weight = []
    results_moment = []
    for slot in range(3):
        weight = weights[slot]
        elements = weight.shape[1] * lax.axis_size("fsdp") * weight.shape[2] * lax.axis_size("tp")
        clip_bound = CLIP_RATIO * jnp.sqrt(jnp.float32(elements))
        clip_factor = jnp.minimum(1.0, clip_bound / jnp.sqrt(totals[slot] + EPS))
        scaled = clip_factor * mixed_all[slot]
        new_moment = BETA * moments[slot] + scaled
        new_weight = (
            weight - GAMMA * (weight - mate_weights[slot]) - RATE * (scaled + BETA * new_moment)
        )
        results_weight.append(new_weight)
        results_moment.append(new_moment)
    return (
        results_weight[0],
        results_weight[1],
        results_weight[2],
        results_moment[0],
        results_moment[1],
        results_moment[2],
    )


def solution(mesh):
    return jax.shard_map(
        local,
        mesh=mesh,
        in_specs=(
            P(),
            P("rep", "fsdp", "tp"),
            P("rep", "fsdp", "tp"),
            P("rep", "fsdp", "tp"),
            P("rep", "fsdp", "tp"),
            P("rep", "fsdp", "tp"),
            P("rep", "fsdp", "tp"),
            P("rep", "fsdp", "tp"),
            P("rep", "fsdp", "tp"),
            P("rep", "fsdp", "tp"),
        ),
        out_specs=(
            P("rep", "fsdp", "tp"),
            P("rep", "fsdp", "tp"),
            P("rep", "fsdp", "tp"),
            P("rep", "fsdp", "tp"),
            P("rep", "fsdp", "tp"),
            P("rep", "fsdp", "tp"),
        ),
        check_vma=False,
    )
```

profile of v0, /device:TPU:1, one launch (start us, length us, event | category | flops | bytes accessed | tf_op | source)
XLA Modules:
  0.0 343.3 jit_solution(7080259094959799865)
XLA Ops:
  3.5 18.4 %all-to-all-start.6 = ((bf16[16,2,640]{2,1,0:T(2,128)(2,1)}), bf16[16,2,640]{2,1,0:T(2,128)(2,1)S(1)}, u32[]{:S(2)}, u32[]{:S(2)}) async-start(bf16[16,2,640]{2,1,0:T(2,128)(2,1)} %reshape.348), calls=%async_computation.6 | async-start | bytes 81920 | tf_op jit(solution)/shard_map/all_to_all | solution.py:42
  22.3 1.8 reduce.3
  24.8 10.8 %all-to-all-done.6 = bf16[16,2,640]{2,1,0:T(2,128)(2,1)S(1)} async-done(((bf16[16,2,640]{2,1,0:T(2,128)(2,1)}), bf16[16,2,640]{2,1,0:T(2,128)(2,1)S(1)}, u32[]{:S(2)}, u32[]{:S(2)}) %all-to-all-start.6) | async-done | bytes 40992 | tf_op jit(solution)/shard_map/all_to_all | solution.py:42
  35.6 3.5 %all-to-all-start.2 = ((bf16[16,2,3200]{2,1,0:T(2,128)(2,1)}), bf16[16,2,3200]{2,1,0:T(2,128)(2,1)S(1)}, u32[]{:S(2)}, u32[]{:S(2)}) async-start(bf16[16,2,3200]{2,1,0:T(2,128)(2,1)} %reshape.356), calls=%async_computation.2 | async-start | bytes 409600 | tf_op jit(solution)/shard_map/all_to_all | solution.py:40
  39.5 1.8 reduce.2
  42.1 12.2 %all-to-all-done.2 = bf16[16,2,3200]{2,1,0:T(2,128)(2,1)S(1)} async-done(((bf16[16,2,3200]{2,1,0:T(2,128)(2,1)}), bf16[16,2,3200]{2,1,0:T(2,128)(2,1)S(1)}, u32[]{:S(2)}, u32[]{:S(2)}) %all-to-all-start.2) | async-done | bytes 204832 | tf_op jit(solution)/shard_map/all_to_all | solution.py:40
  54.3 6.7 %all-to-all-start.4 = ((bf16[16,2,3200]{2,1,0:T(2,128)(2,1)}), bf16[16,2,3200]{2,1,0:T(2,128)(2,1)S(1)}, u32[]{:S(2)}, u32[]{:S(2)}) async-start(bf16[16,2,3200]{2,1,0:T(2,128)(2,1)} %reshape.352), calls=%async_computation.4 | async-start | bytes 409600 | tf_op jit(solution)/shard_map/all_to_all | solution.py:41
  63.1 14.5 %all-to-all-done.4 = bf16[16,2,3200]{2,1,0:T(2,128)(2,1)S(1)} async-done(((bf16[16,2,3200]{2,1,0:T(2,128)(2,1)}), bf16[16,2,3200]{2,1,0:T(2,128)(2,1)S(1)}, u32[]{:S(2)}, u32[]{:S(2)}) %all-to-all-start.4) | async-done | bytes 204832 | tf_op jit(solution)/shard_map/all_to_all | solution.py:41
  77.6 5.5 %all-to-all-start.7 = ((bf16[16,2,640]{2,1,0:T(2,128)(2,1)}), bf16[16,2,640]{2,1,0:T(2,128)(2,1)S(1)}, u32[]{:S(2)}, u32[]{:S(2)}) async-start(bf16[16,2,640]{2,1,0:T(2,128)(2,1)} %reshape.350), calls=%async_computation.7 | async-start | bytes 81920 | tf_op jit(solution)/shard_map/all_to_all | solution.py:56
  85.6 11.2 %all-to-all-done.7 = bf16[16,2,640]{2,1,0:T(2,128)(2,1)S(1)} async-done(((bf16[16,2,640]{2,1,0:T(2,128)(2,1)}), bf16[16,2,640]{2,1,0:T(2,128)(2,1)S(1)}, u32[]{:S(2)}, u32[]{:S(2)}) %all-to-all-start.7) | async-done | bytes 40992 | tf_op jit(solution)/shard_map/all_to_all | solution.py:56
  96.9 3.5 %all-to-all-start.10 = ((f32[1,16,1280]{2,0,1:T(1,128)}), f32[1,16,1280]{2,0,1:T(1,128)S(1)}, u32[]{:S(2)}, u32[]{:S(2)}) async-start(f32[1,16,1280]{2,0,1:T(1,128)} %copy.68), calls=%async_computation.10 | async-start | bytes 163840 | tf_op jit(solution)/shard_map/all_to_all | solution.py:37
  102.0 12.2 %all-to-all-done.10 = f32[1,16,1280]{2,0,1:T(1,128)S(1)} async-done(((f32[1,16,1280]{2,0,1:T(1,128)}), f32[1,16,1280]{2,0,1:T(1,128)S(1)}, u32[]{:S(2)}, u32[]{:S(2)}) %all-to-all-start.10) | async-done | bytes 81952 | tf_op jit(solution)/shard_map/all_to_all | solution.py:37
  114.1 3.5 %all-to-all-start.3 = ((bf16[16,2,3200]{2,1,0:T(2,128)(2,1)}), bf16[16,2,3200]{2,1,0:T(2,128)(2,1)S(1)}, u32[]{:S(2)}, u32[]{:S(2)}) async-start(bf16[16,2,3200]{2,1,0:T(2,128)(2,1)} %reshape.358), calls=%async_computation.3 | async-start | bytes 409600 | tf_op jit(solution)/shard_map/all_to_all | solution.py:54
  119.2 14.7 %all-to-all-done.3 = bf16[16,2,3200]{2,1,0:T(2,128)(2,1)S(1)} async-done(((bf16[16,2,3200]{2,1,0:T(2,128)(2,1)}), bf16[16,2,3200]{2,1,0:T(2,128)(2,1)S(1)}, u32[]{:S(2)}, u32[]{:S(2)}) %all-to-all-start.3) | async-done | bytes 204832 | tf_op jit(solution)/shard_map/all_to_all | solution.py:54
  133.8 3.5 %all-to-all-start.5 = ((bf16[16,2,3200]{2,1,0:T(2,128)(2,1)}), bf16[16,2,3200]{2,1,0:T(2,128)(2,1)S(1)}, u32[]{:S(2)}, u32[]{:S(2)}) async-start(bf16[16,2,3200]{2,1,0:T(2,128)(2,1)} %reshape.354), calls=%async_computation.5 | async-start | bytes 409600 | tf_op jit(solution)/shard_map/all_to_all | solution.py:55
  137.4 1.2 copy.63
  138.5 14.8 %all-to-all-done.5 = bf16[16,2,3200]{2,1,0:T(2,128)(2,1)S(1)} async-done(((bf16[16,2,3200]{2,1,0:T(2,128)(2,1)}), bf16[16,2,3200]{2,1,0:T(2,128)(2,1)S(1)}, u32[]{:S(2)}, u32[]{:S(2)}) %all-to-all-start.5) | async-done | bytes 204832 | tf_op jit(solution)/shard_map/all_to_all | solution.py:55
  153.4 3.6 %all-to-all-start.8 = ((f32[1,16,6400]{2,0,1:T(1,128)}), f32[1,16,6400]{2,0,1:T(1,128)S(1)}, u32[]{:S(2)}, u32[]{:S(2)}) async-start(f32[1,16,6400]{2,0,1:T(1,128)} %copy.63), calls=%async_computation.8 | async-start | bytes 819200 | tf_op jit(solution)/shard_map/all_to_all | solution.py:36
  158.1 14.9 %all-to-all-done.8 = f32[1,16,6400]{2,0,1:T(1,128)S(1)} async-done(((f32[1,16,6400]{2,0,1:T(1,128)}), f32[1,16,6400]{2,0,1:T(1,128)S(1)}, u32[]{:S(2)}, u32[]{:S(2)}) %all-to-all-start.8) | async-done | bytes 409632 | tf_op jit(solution)/shard_map/all_to_all | solution.py:36
  173.0 8.8 %all-to-all-start = ((f32[1,16,6400]{2,0,1:T(1,128)}), f32[1,16,6400]{2,0,1:T(1,128)S(1)}, u32[]{:S(2)}, u32[]{:S(2)}) async-start(f32[1,16,6400]{2,0,1:T(1,128)} %copy.49), calls=%async_computation | async-start | bytes 819200 | tf_op jit(solution)/shard_map/all_to_all | solution.py:35
  185.9 1.4 multiply_reduce_fusion.1
  187.3 1.4 multiply_reduce_fusion
  188.8 2.0 pad_maximum_fusion
  190.8 8.0 %all-to-all-done = f32[1,16,6400]{2,0,1:T(1,128)S(1)} async-done(((f32[1,16,6400]{2,0,1:T(1,128)}), f32[1,16,6400]{2,0,1:T(1,128)S(1)}, u32[]{:S(2)}, u32[]{:S(2)}) %all-to-all-start) | async-done | bytes 409632 | tf_op jit(solution)/shard_map/all_to_all | solution.py:35
  198.8 6.2 %all-to-all-start.11 = ((f32[16,1,1280]{2,1,0:T(1,128)}), f32[16,1,1280]{2,1,0:T(1,128)S(1)}, u32[]{:S(2)}, u32[]{:S(2)}) async-start(f32[16,1,1280]{2,1,0:T(1,128)} %copy.66), calls=%async_computation.11 | async-start | bytes 163840 | tf_op jit(solution)/shard_map/all_to_all | solution.py:51
  205.1 76.8 %psum.7 = f32[3]{0:T(128)S(1)} all-reduce(f32[3]{0:T(128)S(1)} %pad_maximum_fusion), channel_id=1, replica_groups=mesh['rep'=16,'fsdp'=8,'tp'=4] {'fsdp','tp'}, use_global_device_ids=true, to_apply=%region_3.6 | all-reduce | flops 3 | bytes 24 | tf_op jit(solution)/shard_map/psum | solution.py:15
  285.8 13.9 %all-to-all-start.9 = ((f32[16,1,6400]{2,1,0:T(1,128)}), f32[16,1,6400]{2,1,0:T(1,128)S(1)}, u32[]{:S(2)}, u32[]{:S(2)}) async-start(f32[16,1,6400]{2,1,0:T(1,128)} %copy.61), calls=%async_computation.9 | async-start | bytes 819200 | tf_op jit(solution)/shard_map/all_to_all | solution.py:50
  303.4 12.5 %all-to-all-done.9 = f32[16,1,6400]{2,1,0:T(1,128)S(1)} async-done(((f32[16,1,6400]{2,1,0:T(1,128)}), f32[16,1,6400]{2,1,0:T(1,128)S(1)}, u32[]{:S(2)}, u32[]{:S(2)}) %all-to-all-start.9) | async-done | bytes 409632 | tf_op jit(solution)/shard_map/all_to_all | solution.py:50
  315.9 4.8 %all-to-all-start.1 = ((f32[16,1,6400]{2,1,0:T(1,128)}), f32[16,1,6400]{2,1,0:T(1,128)S(1)}, u32[]{:S(2)}, u32[]{:S(2)}) async-start(f32[16,1,6400]{2,1,0:T(1,128)} %copy.47), calls=%async_computation.1 | async-start | bytes 819200 | tf_op jit(solution)/shard_map/all_to_all | solution.py:49
  320.7 2.1 fusion.2
  324.4 15.3 %all-to-all-done.1 = f32[16,1,6400]{2,1,0:T(1,128)S(1)} async-done(((f32[16,1,6400]{2,1,0:T(1,128)}), f32[16,1,6400]{2,1,0:T(1,128)S(1)}, u32[]{:S(2)}, u32[]{:S(2)}) %all-to-all-start.1) | async-done | bytes 409632 | tf_op jit(solution)/shard_map/all_to_all | solution.py:49
  339.6 2.1 fusion.5
  (83 shorter events, 26.3 us)
Async XLA Ops:
  0.6 21.3 %copy-start.1 = (bf16[1,16,6400]{2,1,0:T(8,128)(2,1)S(1)}, bf16[1,16,6400]{2,1,0:T(8,128)(2,1)}, u32[]{:S(2)}) copy-start(bf16[1,16,6400]{2,1,0:T(8,128)(2,1)} %param.21) | copy-start | bytes 614404
  3.5 32.1 %all-to-all-start.6 = ((bf16[16,2,640]{2,1,0:T(2,128)(2,1)}), bf16[16,2,640]{2,1,0:T(2,128)(2,1)S(1)}, u32[]{:S(2)}, u32[]{:S(2)}) async-start(bf16[16,2,640]{2,1,0:T(2,128)(2,1)} %reshape.348), calls=%async_computation.6 | async-start | bytes 81920 | tf_op jit(solution)/shard_map/all_to_all | solution.py:42
  24.8 14.3 %copy-start = (bf16[1,16,6400]{2,1,0:T(8,128)(2,1)S(1)}, bf16[1,16,6400]{2,1,0:T(8,128)(2,1)}, u32[]{:S(2)}) copy-start(bf16[1,16,6400]{2,1,0:T(8,128)(2,1)} %param.22) | copy-start | bytes 614404
  35.6 18.6 %all-to-all-start.2 = ((bf16[16,2,3200]{2,1,0:T(2,128)(2,1)}), bf16[16,2,3200]{2,1,0:T(2,128)(2,1)S(1)}, u32[]{:S(2)}, u32[]{:S(2)}) async-start(bf16[16,2,3200]{2,1,0:T(2,128)(2,1)} %reshape.356), calls=%async_computation.2 | async-start | bytes 409600 | tf_op jit(solution)/shard_map/all_to_all | solution.py:40
  41.3 0.7 copy-start.12
  54.3 23.3 %all-to-all-start.4 = ((bf16[16,2,3200]{2,1,0:T(2,128)(2,1)}), bf16[16,2,3200]{2,1,0:T(2,128)(2,1)S(1)}, u32[]{:S(2)}, u32[]{:S(2)}) async-start(bf16[16,2,3200]{2,1,0:T(2,128)(2,1)} %reshape.352), calls=%async_computation.4 | async-start | bytes 409600 | tf_op jit(solution)/shard_map/all_to_all | solution.py:41
  62.5 20.7 %copy-start.9 = (f32[1,16,1280]{2,1,0:T(8,128)S(1)}, f32[1,16,1280]{2,1,0:T(8,128)}, u32[]{:S(2)}) copy-start(f32[1,16,1280]{2,1,0:T(8,128)} %param.17) | copy-start | bytes 245764
  77.6 19.2 %all-to-all-start.7 = ((bf16[16,2,640]{2,1,0:T(2,128)(2,1)}), bf16[16,2,640]{2,1,0:T(2,128)(2,1)S(1)}, u32[]{:S(2)}, u32[]{:S(2)}) async-start(bf16[16,2,640]{2,1,0:T(2,128)(2,1)} %reshape.350), calls=%async_computation.7 | async-start | bytes 81920 | tf_op jit(solution)/shard_map/all_to_all | solution.py:56
  96.9 17.3 %all-to-all-start.10 = ((f32[1,16,1280]{2,0,1:T(1,128)}), f32[1,16,1280]{2,0,1:T(1,128)S(1)}, u32[]{:S(2)}, u32[]{:S(2)}) async-start(f32[1,16,1280]{2,0,1:T(1,128)} %copy.68), calls=%async_computation.10 | async-start | bytes 163840 | tf_op jit(solution)/shard_map/all_to_all | solution.py:37
  114.1 19.7 %all-to-all-start.3 = ((bf16[16,2,3200]{2,1,0:T(2,128)(2,1)}), bf16[16,2,3200]{2,1,0:T(2,128)(2,1)S(1)}, u32[]{:S(2)}, u32[]{:S(2)}) async-start(bf16[16,2,3200]{2,1,0:T(2,128)(2,1)} %reshape.358), calls=%async_computation.3 | async-start | bytes 409600 | tf_op jit(solution)/shard_map/all_to_all | solution.py:54
  118.4 18.9 %copy-start.2 = (f32[1,16,6400]{2,1,0:T(8,128)S(1)}, f32[1,16,6400]{2,1,0:T(8,128)}, u32[]{:S(2)}) copy-start(f32[1,16,6400]{2,1,0:T(8,128)} %param.16) | copy-start | bytes 1228804
  133.8 19.6 %all-to-all-start.5 = ((bf16[16,2,3200]{2,1,0:T(2,128)(2,1)}), bf16[16,2,3200]{2,1,0:T(2,128)(2,1)S(1)}, u32[]{:S(2)}, u32[]{:S(2)}) async-start(bf16[16,2,3200]{2,1,0:T(2,128)(2,1)} %reshape.354), calls=%async_computation.5 | async-start | bytes 409600 | tf_op jit(solution)/shard_map/all_to_all | solution.py:55
  138.5 18.4 %copy-start.3 = (f32[1,16,6400]{2,1,0:T(8,128)S(1)}, f32[1,16,6400]{2,1,0:T(8,128)}, u32[]{:S(2)}) copy-start(f32[1,16,6400]{2,1,0:T(8,128)} %param.15) | copy-start | bytes 1228804
  153.4 19.7 %all-to-all-start.8 = ((f32[1,16,6400]{2,0,1:T(1,128)}), f32[1,16,6400]{2,0,1:T(1,128)S(1)}, u32[]{:S(2)}, u32[]{:S(2)}) async-start(f32[1,16,6400]{2,0,1:T(1,128)} %copy.63), calls=%async_computation.8 | async-start | bytes 819200 | tf_op jit(solution)/shard_map/all_to_all | solution.py:36
  173.0 25.8 %all-to-all-start = ((f32[1,16,6400]{2,0,1:T(1,128)}), f32[1,16,6400]{2,0,1:T(1,128)S(1)}, u32[]{:S(2)}, u32[]{:S(2)}) async-start(f32[1,16,6400]{2,0,1:T(1,128)} %copy.49), calls=%async_computation | async-start | bytes 819200 | tf_op jit(solution)/shard_map/all_to_all | solution.py:35
  183.3 0.8 copy-start.8
  184.1 0.8 copy-start.4
  198.8 86.9 %all-to-all-start.11 = ((f32[16,1,1280]{2,1,0:T(1,128)}), f32[16,1,1280]{2,1,0:T(1,128)S(1)}, u32[]{:S(2)}, u32[]{:S(2)}) async-start(f32[16,1,1280]{2,1,0:T(1,128)} %copy.66), calls=%async_computation.11 | async-start | bytes 163840 | tf_op jit(solution)/shard_map/all_to_all | solution.py:51
  285.8 30.1 %all-to-all-start.9 = ((f32[16,1,6400]{2,1,0:T(1,128)}), f32[16,1,6400]{2,1,0:T(1,128)S(1)}, u32[]{:S(2)}, u32[]{:S(2)}) async-start(f32[16,1,6400]{2,1,0:T(1,128)} %copy.61), calls=%async_computation.9 | async-start | bytes 819200 | tf_op jit(solution)/shard_map/all_to_all | solution.py:50
  299.7 1.9 copy-start.5
  299.8 1.9 copy-start.10
  299.8 1.9 copy-start.11
  303.4 17.3 %copy-start.6 = (f32[1,16,6400]{2,1,0:T(8,128)S(1)}, f32[1,16,6400]{2,1,0:T(8,128)}, u32[]{:S(2)}) copy-start(f32[1,16,6400]{2,1,0:T(8,128)} %param.19) | copy-start | bytes 1228804
  315.9 23.8 %all-to-all-start.1 = ((f32[16,1,6400]{2,1,0:T(1,128)}), f32[16,1,6400]{2,1,0:T(1,128)S(1)}, u32[]{:S(2)}, u32[]{:S(2)}) async-start(f32[16,1,6400]{2,1,0:T(1,128)} %copy.47), calls=%async_computation.1 | async-start | bytes 819200 | tf_op jit(solution)/shard_map/all_to_all | solution.py:49
  323.6 16.0 %copy-start.7 = (f32[1,16,6400]{2,1,0:T(8,128)S(1)}, f32[1,16,6400]{2,1,0:T(8,128)}, u32[]{:S(2)}) copy-start(f32[1,16,6400]{2,1,0:T(8,128)} %param.18) | copy-start | bytes 1228804
where the time goes:
time: 350 us; the launch traced here: 343 us
  waiting for transfers between devices  141 us (40%)
  starting transfers between devices  81.9 us (23%)
  blocking collectives  76.8 us (22%)
  local copies, waits for them, and re-layouts  22.9 us (7%)
  other arithmetic  17.5 us (5%)
    psum x1, blocking collectives, home_norm(): return lax.psum(partials, ('fsdp', 'tp'))  76.8 us
    all_to_all x1, starting transfers between devices, local(): lax.all_to_all(grad_down, 'rep', split_axis=1, concat_axis=0, tiled=True)  18.4 us
    unnamed x57, local copies, waits for them, and re-layouts  15.3 us
    all_to_all x1, waiting for transfers between devices, local(): lax.all_to_all(paired_weights[0], 'rep', split_axis=0, concat_axis=1, til...  15.3 us
    all_to_all x1, waiting for transfers between devices, local(): lax.all_to_all(weight_up, 'rep', split_axis=1, concat_axis=0, tiled=True)  14.9 us
    all_to_all x1, waiting for transfers between devices, local(): lax.all_to_all(paired_grads[1], 'rep', split_axis=0, concat_axis=1, tiled...  14.8 us
    all_to_all x1, waiting for transfers between devices, local(): lax.all_to_all(paired_grads[0], 'rep', split_axis=0, concat_axis=1, tiled...  14.7 us
    all_to_all x1, waiting for transfers between devices, local(): lax.all_to_all(grad_up, 'rep', split_axis=1, concat_axis=0, tiled=True)  14.5 us
  transfers between devices with their start and end apart: 12, of which 11 were waited for; matrix products, arithmetic and copies ran while one was open for 10% of the time, Pallas kernels for 0%

commit v1 on v0

v1 whole, which is shorter than its diff:
```python
import functools

import jax
import jax.numpy as jnp
from jax import lax
from jax.experimental import pallas as pl
from jax.experimental.pallas import tpu as pltpu
from jax.sharding import PartitionSpec as P

CLIP_RATIO = 0.5
BETA = 0.9
GAMMA = 0.4
RATE = 0.7
EPS = 1e-06

LANES = 128
TOP = 32767.0
STEPS = 16.0
VMEM_LIMIT = 24 * 1024 * 1024


def plan(widths, replicas):
    starts, at = [], 0
    for width in widths:
        count = width // LANES
        starts.append((at, at + count))
        at += 2 * count
    scales = tuple(at + slot for slot in range(3))
    per_home = -(-(at + 3) // replicas)
    return tuple(starts), scales, per_home


def exponent(peak):
    power = jnp.ceil(STEPS * jnp.log2(jnp.maximum(peak, 2.0**-120)))
    return jnp.clip(power, -120.0 * STEPS, 128.0 * STEPS - 1.0)


def encode_kernel(starts, scales, per_home, wg, wu, wd, gg, gu, gd, out):
    rows = wg.shape[1]

    def put(tile, value):
        home, place = divmod(tile, per_home)
        out[home, place * rows : (place + 1) * rows, :] = value

    def coded(block_ref, first):
        count = block_ref.shape[2] // LANES
        peak = jnp.zeros((rows, LANES), jnp.float32)
        for c in range(count):
            peak = jnp.maximum(peak, jnp.abs(block_ref[0, :, c * LANES : (c + 1) * LANES].astype(jnp.float32)))
        power = exponent(jnp.max(peak, axis=(0, 1), keepdims=True))
        factor = jnp.broadcast_to(jnp.exp2(power * (-1.0 / STEPS)), (rows, LANES))
        for c in range(count):
            x = block_ref[0, :, c * LANES : (c + 1) * LANES].astype(jnp.float32)
            level = jnp.minimum(TOP * jnp.sqrt(jnp.abs(x) * factor), TOP) + 0.5
            level = jnp.where(x < 0, -level, level)
            put(first + c, level.astype(jnp.int32).astype(jnp.int16))
        return jnp.broadcast_to(power, (rows, LANES)).astype(jnp.int32)

    upper = lax.broadcasted_iota(jnp.int32, (rows, LANES), 0) < 8
    for slot, (w, g) in enumerate(((wg, gg), (wu, gu), (wd, gd))):
        power_w = coded(w, starts[slot][0])
        power_g = coded(g, starts[slot][1])
        put(scales[slot], jnp.where(upper, power_w, power_g).astype(jnp.int16))
    for tile in range(scales[2] + 1, out.shape[0] * per_home):
        put(tile, jnp.zeros((rows, LANES), jnp.int16))


def swap_kernel(starts, scales, per_home, rows, partner, me, inp, out):
    replicas = inp.shape[0]
    for place in range(per_home):
        tile = me[0] * per_home + place
        slot = jnp.where(tile < starts[1][0], 0, jnp.where(tile < starts[2][0], 1, 2))
        slot = jnp.where(tile == scales[0], 0, jnp.where(tile == scales[1], 1, slot))
        for r in range(replicas):
            source = partner[slot, r]
            out[r, place * rows : (place + 1) * rows, :] = inp[source, place * rows : (place + 1) * rows, :]


def reader(per_home, rows, payload):
    def get(tile):
        home, place = divmod(tile, per_home)
        return payload[home, place * rows : (place + 1) * rows, :].astype(jnp.int32).astype(jnp.float32)

    return get


def decoded(code, scale):
    a = code * (1.0 / TOP)
    return a * jnp.abs(a) * scale


def scales_of(get, tile):
    power = jnp.exp2(get(tile) * (1.0 / STEPS))
    return power[0:1, :], power[8:9, :]


def squares_kernel(starts, scales, per_home, payload, gg, gu, gd, out):
    rows = gg.shape[1]
    get = reader(per_home, rows, payload)
    lane = lax.broadcasted_iota(jnp.int32, (1, LANES), 1)
    total = jnp.zeros((1, LANES), jnp.float32)
    for slot, g in enumerate((gg, gu, gd)):
        _, scale = scales_of(get, scales[slot])
        sums = jnp.zeros((rows, LANES), jnp.float32)
        for c in range(g.shape[2] // LANES):
            own = g[0, :, c * LANES : (c + 1) * LANES].astype(jnp.float32)
            mixed = 0.5 * (own + decoded(get(starts[slot][1] + c), scale))
            sums = sums + mixed * mixed
        total = jnp.where(lane == slot, jnp.sum(sums, axis=(0, 1), keepdims=True), total)
    out[...] = jnp.broadcast_to(total[None], out.shape)


def update_kernel(starts, scales, per_home, elements, sums, payload, wg, wu, wd, mg, mu, md, gg, gu, gd, og, ou, od, ng, nu, nd):
    rows = gg.shape[1]
    get = reader(per_home, rows, payload)
    lane = lax.broadcasted_iota(jnp.int32, (1, LANES), 1)
    totals = jnp.sum(sums[...], axis=0)
    groups = ((wg, mg, gg, og, ng), (wu, mu, gu, ou, nu), (wd, md, gd, od, nd))
    for slot, (w, m, g, o, n) in enumerate(groups):
        scale_w, scale_g = scales_of(get, scales[slot])
        squares = jnp.sum(jnp.where(lane == slot, totals, 0.0), axis=(0, 1), keepdims=True)
        bound = CLIP_RATIO * float(elements[slot]) ** 0.5
        clip = jnp.broadcast_to(jnp.minimum(1.0, bound / jnp.sqrt(squares + EPS)), (rows, LANES))
        for c in range(w.shape[2] // LANES):
            part = slice(c * LANES, (c + 1) * LANES)
            own = g[0, :, part].astype(jnp.float32)
            mixed = 0.5 * (own + decoded(get(starts[slot][1] + c), scale_g))
            mate = decoded(get(starts[slot][0] + c), scale_w)
            scaled = clip * mixed
            moment = BETA * m[0, :, part] + scaled
            weight = w[0, :, part]
            n[0, :, part] = moment
            o[0, :, part] = weight - GAMMA * (weight - mate) - RATE * (scaled + BETA * moment)


def local(partner, wg, wu, wd, mg, mu, md, gg, gu, gd):
    replicas = lax.axis_size("rep")
    shards = lax.axis_size("fsdp") * lax.axis_size("tp")
    rows = wg.shape[1]
    starts, scales, per_home = plan((wg.shape[2], wu.shape[2], wd.shape[2]), replicas)
    params = pltpu.CompilerParams(vmem_limit_bytes=VMEM_LIMIT)
    vmem = pl.BlockSpec(memory_space=pltpu.VMEM)
    smem = pl.BlockSpec(memory_space=pltpu.SMEM)
    packed = jax.ShapeDtypeStruct((replicas, per_home * rows, LANES), jnp.int16)

    coded = pl.pallas_call(
        functools.partial(encode_kernel, starts, scales, per_home),
        out_shape=packed,
        in_specs=[vmem] * 6,
        out_specs=vmem,
        compiler_params=params,
        name="encode",
    )(wg, wu, wd, gg, gu, gd)
    homed = lax.all_to_all(coded, "rep", 0, 0, tiled=True)
    me = lax.axis_index("rep").reshape(1).astype(jnp.int32)
    swapped = pl.pallas_call(
        functools.partial(swap_kernel, starts, scales, per_home, rows),
        out_shape=packed,
        in_specs=[smem, smem, vmem],
        out_specs=vmem,
        compiler_params=params,
        name="swap",
    )(partner, me, homed)
    mates = lax.all_to_all(swapped, "rep", 0, 0, tiled=True)
    partial = pl.pallas_call(
        functools.partial(squares_kernel, starts, scales, per_home),
        out_shape=jax.ShapeDtypeStruct((shards, 1, LANES), jnp.float32),
        in_specs=[vmem] * 4,
        out_specs=vmem,
        compiler_params=params,
        name="squares",
    )(mates, gg, gu, gd)
    sums = lax.all_to_all(partial, ("fsdp", "tp"), 0, 0, tiled=True)
    elements = tuple(shards * w.shape[1] * w.shape[2] for w in (wg, wu, wd))
    arrays = [jax.ShapeDtypeStruct(a.shape, jnp.float32) for a in (wg, wu, wd, mg, mu, md)]
    return pl.pallas_call(
        functools.partial(update_kernel, starts, scales, per_home, elements),
        out_shape=arrays,
        in_specs=[vmem] * 11,
        out_specs=[vmem] * 6,
        compiler_params=params,
        name="update",
    )(sums, mates, wg, wu, wd, mg, mu, md, gg, gu, gd)


def solution(mesh):
    spec = P("rep", "fsdp", "tp")
    return jax.shard_map(
        local,
        mesh=mesh,
        in_specs=(P(),) + (spec,) * 9,
        out_specs=(spec,) * 6,
        check_vma=False,
    )
```

time: 350 us -> 149 us (0.43); the launches traced: 343 us -> 148 us
  waiting for transfers between devices: 141 us -> 39.3 us
  starting transfers between devices: 81.9 us -> 18.4 us
  other arithmetic: 17.5 us -> 0 us
  local copies, waits for them, and re-layouts: 22.9 us -> 5.58 us
  Pallas kernels: 0 us -> 5.48 us
    all_to_all x12 -> x1, waiting for transfers between devices: 141 us -> 39.3 us  [local(): homed = lax.all_to_all(coded, 'rep', 0, 0, tiled=True)]
    all_to_all x0 -> x2, blocking collectives: none -> 78.6 us  [the longest x1 62.6 us: local(): mates = lax.all_to_all(swapped, 'rep', 0, 0, tiled=True)]
    psum x1 -> x0, blocking collectives: 76.8 us -> none  [home_norm(): return lax.psum(partials, ('fsdp', 'tp'))]
    all_to_all x12 -> x1, starting transfers between devices: 81.9 us -> 18.4 us  [local(): homed = lax.all_to_all(coded, 'rep', 0, 0, tiled=True)]
    unnamed x57 -> x32, local copies, waits for them, and re-layouts: 15.3 us -> 5.58 us
    pallas_call x0 -> x4, Pallas kernels: none -> 5.48 us  [the longest x1 2.31 us: local(): pl.pallas_call(functools.partial(encode_kernel, starts, scales, per_home)...]
    sub x3 -> x0, other arithmetic: 4.64 us -> none  [local(): weight - GAMMA * (weight - mate_weights[slot])]
    unnamed x3 -> x0, other arithmetic: 4.51 us -> none
  transfers between devices with their start and end apart: 12 -> 1, of which waited for: 11 -> 1; matrix products, arithmetic and copies ran while one was open for 10% -> 0% of each run, Pallas kernels for 0% -> 0%
where the time goes in v1:
time: 149 us; the launch traced here: 148 us
  blocking collectives  78.6 us (53%)
  waiting for transfers between devices  39.3 us (26%)
  starting transfers between devices  18.4 us (12%)
  local copies, waits for them, and re-layouts  5.58 us (4%)
  Pallas kernels  5.48 us (4%)
    all_to_all x1, blocking collectives, local(): mates = lax.all_to_all(swapped, 'rep', 0, 0, tiled=True)  62.6 us
    all_to_all x1, waiting for transfers between devices, local(): homed = lax.all_to_all(coded, 'rep', 0, 0, tiled=True)  39.3 us
    all_to_all x1, starting transfers between devices, local(): homed = lax.all_to_all(coded, 'rep', 0, 0, tiled=True)  18.4 us
    all_to_all x1, blocking collectives, local(): sums = lax.all_to_all(partial, ('fsdp', 'tp'), 0, 0, tiled=True)  15.9 us
    unnamed x32, local copies, waits for them, and re-layouts  5.58 us
  transfers between devices with their start and end apart: 1, of which 1 were waited for; matrix products, arithmetic and copies ran while one was open for 0% of the time, Pallas kernels for 0%

profile of v1, /device:TPU:1, one launch (start us, length us, event | category | flops | bytes accessed | tf_op | source)
XLA Modules:
  0.0 148.1 jit_solution(14183269114649346333)
XLA Ops:
  0.6 0.0 copy-start
  0.6 0.9 copy-done
  1.6 0.9 copy-done.2
  2.5 1.0 copy-done.4
  3.5 1.0 copy-done.6
  4.5 0.8 copy-done.10
  5.3 0.9 copy-done.12
  6.2 2.3 %encode.1 = s16[16,224,128]{2,1,0:T(8,128)(2,1)} custom-call(f32[1,16,6400]{2,1,0:T(8,128)S(1)} %copy-done.4, f32[1,16,6400]{2,1,0:T(8,128)S(1)} %copy-done.6, f32[1,16,1280]{2,1,0:T(8,128)S(1)} %copy-done.12, bf16[1,16,6400]{2,1,0:T(8,128)(2,1)S(1)} %copy-done, bf16[1,16,6400]{2,1,0:T(8,128)(2,1)S(1)} %copy-done.2, bf16[1,16,1280]{2,1,0:T(8,128)(2,1)S(1)} %copy-done.10), custom_call_target="tpu_custom_call" | custom-call | tf_op jit(solution)/shard_map/encode/pallas_call | solution.py:146
  8.5 18.4 %all-to-all-start = ((s16[16,224,128]{2,1,0:T(8,128)(2,1)}), s16[16,224,128]{2,1,0:T(8,128)(2,1)S(1)}, u32[]{:S(2)}, u32[]{:S(2)}) async-start(s16[16,224,128]{2,1,0:T(8,128)(2,1)} %encode.1), calls=%async_computation | async-start | bytes 1835008 | tf_op jit(solution)/shard_map/all_to_all | solution.py:154
  26.9 0.0 copy-start.15
  26.9 39.3 %all-to-all-done.inp = s16[16,224,128]{2,1,0:T(8,128)(2,1)S(1)} async-done(((s16[16,224,128]{2,1,0:T(8,128)(2,1)}), s16[16,224,128]{2,1,0:T(8,128)(2,1)S(1)}, u32[]{:S(2)}, u32[]{:S(2)}) %all-to-all-start) | async-done | bytes 917536 | tf_op jit(solution)/shard_map/all_to_all | solution.py:154
  66.2 0.0 copy-done.15
  66.2 0.8 swap.1
  67.0 0.0 copy-start.1
  67.0 0.0 copy-start.3
  67.0 0.0 copy-start.11
  67.0 0.0 copy-start.9
  67.1 62.6 %all_to_all.15.payload = s16[16,224,128]{2,1,0:T(8,128)(2,1)S(1)} all-to-all(s16[16,224,128]{2,1,0:T(8,128)(2,1)S(1)} %swap.1), channel_id=1, replica_groups=mesh['rep'=16,'fsdp'=8,'tp'=4] {'rep'}, dimensions={0} | all-to-all | bytes 1835008 | tf_op jit(solution)/shard_map/all_to_all | solution.py:164
  129.7 0.0 copy-done.1
  129.7 0.0 copy-done.3
  129.7 0.0 copy-done.11
  129.7 0.0 copy-start.5
  129.7 0.0 copy-start.7
  129.7 0.0 copy-start.8
  129.7 0.0 copy-start.13
  129.8 0.0 copy-start.14
  129.8 0.5 squares.1
  130.2 15.9 %all_to_all.16.sums = f32[32,1,128]{2,1,0:T(1,128)S(1)} all-to-all(f32[32,1,128]{2,1,0:T(1,128)S(1)} %squares.1), channel_id=1, replica_groups=mesh['rep'=16,'fsdp'=8,'tp'=4] {'fsdp','tp'}, dimensions={0} | all-to-all | bytes 32768 | tf_op jit(solution)/shard_map/all_to_all | solution.py:173
  146.2 0.0 copy-done.8
  146.2 0.0 copy-done.13
  146.2 0.0 copy-done.14
  146.2 1.9 %update.1 = (f32[1,16,6400]{2,1,0:T(8,128)}, f32[1,16,6400]{2,1,0:T(8,128)}, f32[1,16,1280]{2,1,0:T(8,128)}, f32[1,16,6400]{2,1,0:T(8,128)}, f32[1,16,6400]{2,1,0:T(8,128)}, /*index=5*/f32[1,16,1280]{2,1,0:T(8,128)}) custom-call(f32[32,1,128]{2,1,0:T(1,128)S(1)} %all_to_all.16.sums, s16[16,224,128]{2,1,0:T(8,128)(2,1)S(1)} %all_to_all.15.payload, ...), custom_call_target="tpu_custom_call" | custom-call | tf_op jit(solution)/shard_map/update/pallas_call | solution.py:176
  (8 shorter events, 0.0 us)
Async XLA Ops:
  0.6 0.9 copy-start
  1.6 0.9 copy-start.2
  2.5 1.0 copy-start.4
  3.5 1.0 copy-start.6
  4.5 0.8 copy-start.10
  5.3 0.9 copy-start.12
  8.5 57.7 %all-to-all-start = ((s16[16,224,128]{2,1,0:T(8,128)(2,1)}), s16[16,224,128]{2,1,0:T(8,128)(2,1)S(1)}, u32[]{:S(2)}, u32[]{:S(2)}) async-start(s16[16,224,128]{2,1,0:T(8,128)(2,1)} %encode.1), calls=%async_computation | async-start | bytes 1835008 | tf_op jit(solution)/shard_map/all_to_all | solution.py:154
  26.9 39.3 %copy-start.15 = (s32[3,16]{1,0:T(4,128)S(1)}, s32[3,16]{1,0:T(4,128)}, u32[]{:S(2)}) copy-start(s32[3,16]{1,0:T(4,128)} %partner.1) | copy-start | bytes 580
  67.0 62.7 %copy-start.1 = (bf16[1,16,6400]{2,1,0:T(8,128)(2,1)S(1)}, bf16[1,16,6400]{2,1,0:T(8,128)(2,1)}, u32[]{:S(2)}) copy-start(bf16[1,16,6400]{2,1,0:T(8,128)(2,1)} %gg.5) | copy-start | bytes 614404
  67.0 62.7 %copy-start.3 = (bf16[1,16,6400]{2,1,0:T(8,128)(2,1)S(1)}, bf16[1,16,6400]{2,1,0:T(8,128)(2,1)}, u32[]{:S(2)}) copy-start(bf16[1,16,6400]{2,1,0:T(8,128)(2,1)} %gu.5) | copy-start | bytes 614404
  67.0 62.7 %copy-start.11 = (bf16[1,16,1280]{2,1,0:T(8,128)(2,1)S(1)}, bf16[1,16,1280]{2,1,0:T(8,128)(2,1)}, u32[]{:S(2)}) copy-start(bf16[1,16,1280]{2,1,0:T(8,128)(2,1)} %gd.5) | copy-start | bytes 122884
  67.0 79.1 %copy-start.9 = (f32[1,16,6400]{2,1,0:T(8,128)S(1)}, f32[1,16,6400]{2,1,0:T(8,128)}, u32[]{:S(2)}) copy-start(f32[1,16,6400]{2,1,0:T(8,128)} %mu.1) | copy-start | bytes 1228804
  129.7 16.5 %copy-start.5 = (f32[1,16,6400]{2,1,0:T(8,128)S(1)}, f32[1,16,6400]{2,1,0:T(8,128)}, u32[]{:S(2)}) copy-start(f32[1,16,6400]{2,1,0:T(8,128)} %wg.3) | copy-start | bytes 1228804
  129.7 16.4 %copy-start.7 = (f32[1,16,6400]{2,1,0:T(8,128)S(1)}, f32[1,16,6400]{2,1,0:T(8,128)}, u32[]{:S(2)}) copy-start(f32[1,16,6400]{2,1,0:T(8,128)} %wu.3) | copy-start | bytes 1228804
  129.7 16.4 %copy-start.8 = (f32[1,16,6400]{2,1,0:T(8,128)S(1)}, f32[1,16,6400]{2,1,0:T(8,128)}, u32[]{:S(2)}) copy-start(f32[1,16,6400]{2,1,0:T(8,128)} %mg.1) | copy-start | bytes 1228804
  129.7 16.4 %copy-start.13 = (f32[1,16,1280]{2,1,0:T(8,128)S(1)}, f32[1,16,1280]{2,1,0:T(8,128)}, u32[]{:S(2)}) copy-start(f32[1,16,1280]{2,1,0:T(8,128)} %wd.3) | copy-start | bytes 245764
  129.8 16.4 %copy-start.14 = (f32[1,16,1280]{2,1,0:T(8,128)S(1)}, f32[1,16,1280]{2,1,0:T(8,128)}, u32[]{:S(2)}) copy-start(f32[1,16,1280]{2,1,0:T(8,128)} %md.1) | copy-start | bytes 245764

commit v2 on v1

--- a/solution.py
+++ b/solution.py
@@ -17,6 +17,7 @@
 TOP = 32767.0
 STEPS = 16.0
 VMEM_LIMIT = 24 * 1024 * 1024
+ENCODE_LIMIT = 60 * 1024 * 1024
 
 
 def plan(widths, replicas):
@@ -35,8 +36,12 @@
     return jnp.clip(power, -120.0 * STEPS, 128.0 * STEPS - 1.0)
 
 
-def encode_kernel(starts, scales, per_home, wg, wu, wd, gg, gu, gd, out):
+def encode_kernel(starts, scales, per_home, wg, wu, wd, gg, gu, gd, out, vwg, vwu, vwd, vgg, vgu, vgd, sems):
     rows = wg.shape[1]
+    pairs = ((wd, vwd), (gd, vgd), (wg, vwg), (gg, vgg), (wu, vwu), (gu, vgu))
+    copies = [pltpu.make_async_copy(src, dst, sems.at[i]) for i, (src, dst) in enumerate(pairs)]
+    for copy in copies:
+        copy.start()
 
     def put(tile, value):
         home, place = divmod(tile, per_home)
@@ -56,13 +61,15 @@
             put(first + c, level.astype(jnp.int32).astype(jnp.int16))
         return jnp.broadcast_to(power, (rows, LANES)).astype(jnp.int32)
 
+    for tile in range(scales[2] + 1, out.shape[0] * per_home):
+        put(tile, jnp.zeros((rows, LANES), jnp.int16))
     upper = lax.broadcasted_iota(jnp.int32, (rows, LANES), 0) < 8
-    for slot, (w, g) in enumerate(((wg, gg), (wu, gu), (wd, gd))):
+    for at, (slot, w, g) in enumerate(((2, vwd, vgd), (0, vwg, vgg), (1, vwu, vgu))):
+        copies[2 * at].wait()
         power_w = coded(w, starts[slot][0])
+        copies[2 * at + 1].wait()
         power_g = coded(g, starts[slot][1])
         put(scales[slot], jnp.where(upper, power_w, power_g).astype(jnp.int16))
-    for tile in range(scales[2] + 1, out.shape[0] * per_home):
-        put(tile, jnp.zeros((rows, LANES), jnp.int16))
 
 
 def swap_kernel(starts, scales, per_home, rows, partner, me, inp, out):
@@ -146,9 +153,10 @@
     coded = pl.pallas_call(
         functools.partial(encode_kernel, starts, scales, per_home),
         out_shape=packed,
-        in_specs=[vmem] * 6,
+        in_specs=[pl.BlockSpec(memory_space=pl.ANY)] * 6,
         out_specs=vmem,
-        compiler_params=params,
+        scratch_shapes=[pltpu.VMEM(a.shape, a.dtype) for a in (wg, wu, wd, gg, gu, gd)] + [pltpu.SemaphoreType.DMA((6,))],
+        compiler_params=pltpu.CompilerParams(vmem_limit_bytes=ENCODE_LIMIT),
         name="encode",
     )(wg, wu, wd, gg, gu, gd)
     homed = lax.all_to_all(coded, "rep", 0, 0, tiled=True)

time: 149 us -> 145 us (0.973)
  local copies, waits for them, and re-layouts: 5.58 us -> 0.06 us
  Pallas kernels: 5.48 us -> 7.18 us
    unnamed x32 -> x20, local copies, waits for them, and re-layouts: 5.58 us -> 0.06 us
    pallas_call x1, Pallas kernels: 2.31 us -> 4.01 us  [local(): pl.pallas_call(functools.partial(encode_kernel, starts, scales, per_home)...]
where the time goes in v2:
time: 145 us; the launch traced here: 144 us
  blocking collectives  78.6 us (54%)
  waiting for transfers between devices  39.3 us (27%)
  starting transfers between devices  18.4 us (13%)
  Pallas kernels  7.18 us (5%)
    all_to_all x1, blocking collectives, local(): mates = lax.all_to_all(swapped, 'rep', 0, 0, tiled=True)  62.6 us
    all_to_all x1, waiting for transfers between devices, local(): homed = lax.all_to_all(coded, 'rep', 0, 0, tiled=True)  39.3 us
    all_to_all x1, starting transfers between devices, local(): homed = lax.all_to_all(coded, 'rep', 0, 0, tiled=True)  18.4 us
    all_to_all x1, blocking collectives, local(): sums = lax.all_to_all(partial, ('fsdp', 'tp'), 0, 0, tiled=True)  15.9 us
    pallas_call x1, Pallas kernels, local(): pl.pallas_call(functools.partial(encode_kernel, starts, scales, per_home)...  4.01 us
  transfers between devices with their start and end apart: 1, of which 1 were waited for; matrix products, arithmetic and copies ran while one was open for 0% of the time, Pallas kernels for 0%

profile of v2, /device:TPU:1, one launch (start us, length us, event | category | flops | bytes accessed | tf_op | source)
XLA Modules:
  0.0 144.2 jit_solution(10999366555967347872)
XLA Ops:
  0.6 4.0 %encode.1 = s16[16,224,128]{2,1,0:T(8,128)(2,1)} custom-call(f32[1,16,6400]{2,1,0:T(8,128)} %wg.3, f32[1,16,6400]{2,1,0:T(8,128)} %wu.3, f32[1,16,1280]{2,1,0:T(8,128)} %wd.3, bf16[1,16,6400]{2,1,0:T(8,128)(2,1)} %gg.5, bf16[1,16,6400]{2,1,0:T(8,128)(2,1)} %gu.5, bf16[1,16,1280]{2,1,0:T(8,128)(2,1)} %gd.5), custom_call_target="tpu_custom_call" | custom-call | tf_op jit(solution)/shard_map/encode/pallas_call | solution.py:153
  4.6 18.4 %all-to-all-start = ((s16[16,224,128]{2,1,0:T(8,128)(2,1)}), s16[16,224,128]{2,1,0:T(8,128)(2,1)S(1)}, u32[]{:S(2)}, u32[]{:S(2)}) async-start(s16[16,224,128]{2,1,0:T(8,128)(2,1)} %encode.1), calls=%async_computation | async-start | bytes 1835008 | tf_op jit(solution)/shard_map/all_to_all | solution.py:162
  23.0 0.0 copy-start.9
  23.1 39.3 %all-to-all-done.inp = s16[16,224,128]{2,1,0:T(8,128)(2,1)S(1)} async-done(((s16[16,224,128]{2,1,0:T(8,128)(2,1)}), s16[16,224,128]{2,1,0:T(8,128)(2,1)S(1)}, u32[]{:S(2)}, u32[]{:S(2)}) %all-to-all-start) | async-done | bytes 917536 | tf_op jit(solution)/shard_map/all_to_all | solution.py:162
  62.3 0.0 copy-done.9
  62.3 0.8 swap.1
  63.2 0.0 copy-start
  63.2 0.0 copy-start.1
  63.2 0.0 copy-start.6
  63.2 0.0 copy-start.5
  63.2 62.6 %all_to_all.15.payload = s16[16,224,128]{2,1,0:T(8,128)(2,1)S(1)} all-to-all(s16[16,224,128]{2,1,0:T(8,128)(2,1)S(1)} %swap.1), channel_id=1, replica_groups=mesh['rep'=16,'fsdp'=8,'tp'=4] {'rep'}, dimensions={0} | all-to-all | bytes 1835008 | tf_op jit(solution)/shard_map/all_to_all | solution.py:172
  125.9 0.0 copy-done
  125.9 0.0 copy-done.1
  125.9 0.0 copy-done.6
  125.9 0.0 copy-start.2
  125.9 0.0 copy-start.3
  125.9 0.0 copy-start.4
  125.9 0.0 copy-start.7
  125.9 0.0 copy-start.8
  125.9 0.5 squares.1
  126.4 15.9 %all_to_all.16.sums = f32[32,1,128]{2,1,0:T(1,128)S(1)} all-to-all(f32[32,1,128]{2,1,0:T(1,128)S(1)} %squares.1), channel_id=1, replica_groups=mesh['rep'=16,'fsdp'=8,'tp'=4] {'fsdp','tp'}, dimensions={0} | all-to-all | bytes 32768 | tf_op jit(solution)/shard_map/all_to_all | solution.py:181
  142.3 0.0 copy-done.5
  142.3 0.0 copy-done.2
  142.3 0.0 copy-done.3
  142.3 0.0 copy-done.4
  142.4 0.0 copy-done.7
  142.4 0.0 copy-done.8
  142.4 1.9 %update.1 = (f32[1,16,6400]{2,1,0:T(8,128)}, f32[1,16,6400]{2,1,0:T(8,128)}, f32[1,16,1280]{2,1,0:T(8,128)}, f32[1,16,6400]{2,1,0:T(8,128)}, f32[1,16,6400]{2,1,0:T(8,128)}, /*index=5*/f32[1,16,1280]{2,1,0:T(8,128)}) custom-call(f32[32,1,128]{2,1,0:T(1,128)S(1)} %all_to_all.16.sums, s16[16,224,128]{2,1,0:T(8,128)(2,1)S(1)} %all_to_all.15.payload, ...), custom_call_target="tpu_custom_call" | custom-call | tf_op jit(solution)/shard_map/update/pallas_call | solution.py:184
Async XLA Ops:
  4.6 57.7 %all-to-all-start = ((s16[16,224,128]{2,1,0:T(8,128)(2,1)}), s16[16,224,128]{2,1,0:T(8,128)(2,1)S(1)}, u32[]{:S(2)}, u32[]{:S(2)}) async-start(s16[16,224,128]{2,1,0:T(8,128)(2,1)} %encode.1), calls=%async_computation | async-start | bytes 1835008 | tf_op jit(solution)/shard_map/all_to_all | solution.py:162
  23.0 39.3 %copy-start.9 = (s32[3,16]{1,0:T(4,128)S(1)}, s32[3,16]{1,0:T(4,128)}, u32[]{:S(2)}) copy-start(s32[3,16]{1,0:T(4,128)} %partner.1) | copy-start | bytes 580
  63.2 62.7 %copy-start = (bf16[1,16,6400]{2,1,0:T(8,128)(2,1)S(1)}, bf16[1,16,6400]{2,1,0:T(8,128)(2,1)}, u32[]{:S(2)}) copy-start(bf16[1,16,6400]{2,1,0:T(8,128)(2,1)} %gg.5) | copy-start | bytes 614404
  63.2 62.7 %copy-start.1 = (bf16[1,16,6400]{2,1,0:T(8,128)(2,1)S(1)}, bf16[1,16,6400]{2,1,0:T(8,128)(2,1)}, u32[]{:S(2)}) copy-start(bf16[1,16,6400]{2,1,0:T(8,128)(2,1)} %gu.5) | copy-start | bytes 614404
  63.2 62.7 %copy-start.6 = (bf16[1,16,1280]{2,1,0:T(8,128)(2,1)S(1)}, bf16[1,16,1280]{2,1,0:T(8,128)(2,1)}, u32[]{:S(2)}) copy-start(bf16[1,16,1280]{2,1,0:T(8,128)(2,1)} %gd.5) | copy-start | bytes 122884
  63.2 79.1 %copy-start.5 = (f32[1,16,6400]{2,1,0:T(8,128)S(1)}, f32[1,16,6400]{2,1,0:T(8,128)}, u32[]{:S(2)}) copy-start(f32[1,16,6400]{2,1,0:T(8,128)} %mu.1) | copy-start | bytes 1228804
  125.9 16.5 %copy-start.2 = (f32[1,16,6400]{2,1,0:T(8,128)S(1)}, f32[1,16,6400]{2,1,0:T(8,128)}, u32[]{:S(2)}) copy-start(f32[1,16,6400]{2,1,0:T(8,128)} %wg.3) | copy-start | bytes 1228804
  125.9 16.4 %copy-start.3 = (f32[1,16,6400]{2,1,0:T(8,128)S(1)}, f32[1,16,6400]{2,1,0:T(8,128)}, u32[]{:S(2)}) copy-start(f32[1,16,6400]{2,1,0:T(8,128)} %wu.3) | copy-start | bytes 1228804
  125.9 16.4 %copy-start.4 = (f32[1,16,6400]{2,1,0:T(8,128)S(1)}, f32[1,16,6400]{2,1,0:T(8,128)}, u32[]{:S(2)}) copy-start(f32[1,16,6400]{2,1,0:T(8,128)} %mg.1) | copy-start | bytes 1228804
  125.9 16.4 %copy-start.7 = (f32[1,16,1280]{2,1,0:T(8,128)S(1)}, f32[1,16,1280]{2,1,0:T(8,128)}, u32[]{:S(2)}) copy-start(f32[1,16,1280]{2,1,0:T(8,128)} %wd.3) | copy-start | bytes 245764
  125.9 16.4 %copy-start.8 = (f32[1,16,1280]{2,1,0:T(8,128)S(1)}, f32[1,16,1280]{2,1,0:T(8,128)}, u32[]{:S(2)}) copy-start(f32[1,16,1280]{2,1,0:T(8,128)} %md.1) | copy-start | bytes 245764

commit v3 on v2

--- a/solution.py
+++ b/solution.py
@@ -31,13 +31,23 @@
     return tuple(starts), scales, per_home
 
 
+def locate(parts, cuts, place):
+    for part, cut in zip(parts, cuts):
+        if place < cut:
+            return part, place
+        place -= cut
+    raise ValueError("place")
+
+
 def exponent(peak):
     power = jnp.ceil(STEPS * jnp.log2(jnp.maximum(peak, 2.0**-120)))
     return jnp.clip(power, -120.0 * STEPS, 128.0 * STEPS - 1.0)
 
 
-def encode_kernel(starts, scales, per_home, wg, wu, wd, gg, gu, gd, out, vwg, vwu, vwd, vgg, vgu, vgd, sems):
+def encode_kernel(starts, scales, cuts, wg, wu, wd, gg, gu, gd, *refs):
+    outs, (vwg, vwu, vwd, vgg, vgu, vgd, sems) = refs[: len(cuts)], refs[len(cuts) :]
     rows = wg.shape[1]
+    per_home = sum(cuts)
     pairs = ((wd, vwd), (gd, vgd), (wg, vwg), (gg, vgg), (wu, vwu), (gu, vgu))
     copies = [pltpu.make_async_copy(src, dst, sems.at[i]) for i, (src, dst) in enumerate(pairs)]
     for copy in copies:
@@ -45,6 +55,7 @@
 
     def put(tile, value):
         home, place = divmod(tile, per_home)
+        out, place = locate(outs, cuts, place)
         out[home, place * rows : (place + 1) * rows, :] = value
 
     def coded(block_ref, first):
@@ -61,7 +72,7 @@
             put(first + c, level.astype(jnp.int32).astype(jnp.int16))
         return jnp.broadcast_to(power, (rows, LANES)).astype(jnp.int32)
 
-    for tile in range(scales[2] + 1, out.shape[0] * per_home):
+    for tile in range(scales[2] + 1, outs[0].shape[0] * per_home):
         put(tile, jnp.zeros((rows, LANES), jnp.int16))
     upper = lax.broadcasted_iota(jnp.int32, (rows, LANES), 0) < 8
     for at, (slot, w, g) in enumerate(((2, vwd, vgd), (0, vwg, vgg), (1, vwu, vgu))):
@@ -72,15 +83,18 @@
         put(scales[slot], jnp.where(upper, power_w, power_g).astype(jnp.int16))
 
 
-def swap_kernel(starts, scales, per_home, rows, partner, me, inp, out):
-    replicas = inp.shape[0]
+def swap_kernel(starts, scales, cuts, rows, partner, me, *refs):
+    inps, out = refs[:-1], refs[-1]
+    replicas = out.shape[0]
+    per_home = sum(cuts)
     for place in range(per_home):
         tile = me[0] * per_home + place
         slot = jnp.where(tile < starts[1][0], 0, jnp.where(tile < starts[2][0], 1, 2))
         slot = jnp.where(tile == scales[0], 0, jnp.where(tile == scales[1], 1, slot))
+        inp, at = locate(inps, cuts, place)
         for r in range(replicas):
             source = partner[slot, r]
-            out[r, place * rows : (place + 1) * rows, :] = inp[source, place * rows : (place + 1) * rows, :]
+            out[r, place * rows : (place + 1) * rows, :] = inp[source, at * rows : (at + 1) * rows, :]
 
 
 def reader(per_home, rows, payload):
@@ -150,25 +164,39 @@
     smem = pl.BlockSpec(memory_space=pltpu.SMEM)
     packed = jax.ShapeDtypeStruct((replicas, per_home * rows, LANES), jnp.int16)
 
-    coded = pl.pallas_call(
-        functools.partial(encode_kernel, starts, scales, per_home),
-        out_shape=packed,
-        in_specs=[pl.BlockSpec(memory_space=pl.ANY)] * 6,
-        out_specs=vmem,
-        scratch_shapes=[pltpu.VMEM(a.shape, a.dtype) for a in (wg, wu, wd, gg, gu, gd)] + [pltpu.SemaphoreType.DMA((6,))],
-        compiler_params=pltpu.CompilerParams(vmem_limit_bytes=ENCODE_LIMIT),
-        name="encode",
-    )(wg, wu, wd, gg, gu, gd)
-    homed = lax.all_to_all(coded, "rep", 0, 0, tiled=True)
     me = lax.axis_index("rep").reshape(1).astype(jnp.int32)
-    swapped = pl.pallas_call(
-        functools.partial(swap_kernel, starts, scales, per_home, rows),
-        out_shape=packed,
-        in_specs=[smem, smem, vmem],
-        out_specs=vmem,
-        compiler_params=params,
-        name="swap",
-    )(partner, me, homed)
+
+    def outward(cuts, *operands):
+        coded = pl.pallas_call(
+            functools.partial(encode_kernel, starts, scales, cuts),
+            out_shape=[jax.ShapeDtypeStruct((replicas, cut * rows, LANES), jnp.int16) for cut in cuts],
+            in_specs=[pl.BlockSpec(memory_space=pl.ANY)] * 6,
+            out_specs=[vmem] * len(cuts),
+            scratch_shapes=[pltpu.VMEM(a.shape, a.dtype) for a in operands[2:]] + [pltpu.SemaphoreType.DMA((6,))],
+            compiler_params=pltpu.CompilerParams(vmem_limit_bytes=ENCODE_LIMIT),
+            name="encode",
+        )(*operands[2:])
+        coded = list(coded)
+        homed = []
+        for i in range(len(cuts)):
+            homed.append(lax.all_to_all(coded[i], "rep", 0, 0, tiled=True))
+            if i + 1 < len(cuts):
+                homed[i], coded[i + 1] = lax.optimization_barrier((homed[i], coded[i + 1]))
+        return pl.pallas_call(
+            functools.partial(swap_kernel, starts, scales, cuts, rows),
+            out_shape=packed,
+            in_specs=[smem, smem] + [vmem] * len(cuts),
+            out_specs=vmem,
+            compiler_params=params,
+            name="swap",
+        )(operands[0], operands[1], *homed)
+
+    swapped = lax.cond(
+        lax.rem(lax.axis_index("fsdp"), 2) == 1,
+        functools.partial(outward, (1, per_home - 1)),
+        functools.partial(outward, (per_home,)),
+        partner, me, wg, wu, wd, gg, gu, gd,
+    )
     mates = lax.all_to_all(swapped, "rep", 0, 0, tiled=True)
     partial = pl.pallas_call(
         functools.partial(squares_kernel, starts, scales, per_home),

time: 145 us -> 135 us (0.931)
  blocking collectives: 78.6 us -> 126 us
  waiting for transfers between devices: 39.3 us -> 0 us
  starting transfers between devices: 18.4 us -> 0 us
    all_to_all x0 -> x2, blocking collectives: none -> 69.9 us  [outward(): homed.append(lax.all_to_all(coded[i], 'rep', 0, 0, tiled=True))]
    all_to_all x1 -> x0, waiting for transfers between devices: 39.3 us -> none  [local(): homed = lax.all_to_all(coded, 'rep', 0, 0, tiled=True)]
    all_to_all x1, blocking collectives: 62.6 us -> 43.6 us  [local(): mates = lax.all_to_all(swapped, 'rep', 0, 0, tiled=True)]
    all_to_all x1 -> x0, starting transfers between devices: 18.4 us -> none  [local(): homed = lax.all_to_all(coded, 'rep', 0, 0, tiled=True)]
    all_to_all x1, blocking collectives: 15.9 us -> 12.9 us  [local(): sums = lax.all_to_all(partial, ('fsdp', 'tp'), 0, 0, tiled=True)]
  transfers between devices with their start and end apart: 1 -> 0, of which waited for: 1 -> 0; matrix products, arithmetic and copies ran while one was open for 0% -> 0% of each run, Pallas kernels for 0% -> 0%
where the time goes in v3:
time: 135 us
  blocking collectives  126 us (93%)
  Pallas kernels  7.16 us (5%)
    all_to_all x2, blocking collectives, outward(): homed.append(lax.all_to_all(coded[i], 'rep', 0, 0, tiled=True))  69.9 us
    all_to_all x1, blocking collectives, local(): mates = lax.all_to_all(swapped, 'rep', 0, 0, tiled=True)  43.6 us
    all_to_all x1, blocking collectives, local(): sums = lax.all_to_all(partial, ('fsdp', 'tp'), 0, 0, tiled=True)  12.9 us
    pallas_call x1, Pallas kernels, outward(): pl.pallas_call(functools.partial(encode_kernel, starts, scales, cuts), ou...  4 us

profile of v3, /device:TPU:1, one launch (start us, length us, event | category | flops | bytes accessed | tf_op | source)
XLA Modules:
  0.0 135.1 jit_solution(3656913570718869669)
XLA Ops:
  0.6 0.0 copy-start.9
  0.6 0.7 copy-done.9
  1.3 74.7 %conditional.1 = (s16[16,224,128]{2,1,0:T(8,128)(2,1)S(1)}) conditional(s32[]{:T(128)} %convert_element_type.3, (f32[1,16,6400]{2,1,0:T(8,128)}, f32[1,16,6400]{2,1,0:T(8,128)}, f32[1,16,1280]{2,1,0:T(8,128)}, bf16[1,16,6400]{2,1,0:T(8,128)(2,1)}, bf16[1,16,6400]{2,1,0:T(8,128)(2,1)}, /*index=5*/bf16[1,16,1280]{2,1,0:T(8,128)(2,1)}, ...), branch_computations={%region_0.0_spmd, %region_1.0_spmd} | conditional | bytes 1835016 | solution.py:194
  1.3 4.0 %encode.3 = (s16[16,16,128]{2,1,0:T(8,128)(2,1)}, s16[16,208,128]{2,1,0:T(8,128)(2,1)}) custom-call(f32[1,16,6400]{2,1,0:T(8,128)} %get-tuple-element.45.wg, f32[1,16,6400]{2,1,0:T(8,128)} %get-tuple-element.46.wu, f32[1,16,1280]{2,1,0:T(8,128)} %get-tuple-element.47.wd, bf16[1,16,6400]{2,1,0:T(8,128)(2,1)} %get-tuple-element.48.gg, ...), custom_call_target="tpu_custom_call" | custom-call | tf_op jit(solution)/shard_map/cond/branch_1_fun/encode/pallas_call | solution.py:170
  5.3 32.3 %all_to_all.23.refs_0_ = s16[16,16,128]{2,1,0:T(8,128)(2,1)S(1)} all-to-all(s16[16,16,128]{2,1,0:T(8,128)(2,1)} %get-tuple-element.51), channel_id=1, replica_groups=mesh['rep'=16,'fsdp'=8,'tp'=4] {'rep'}, dimensions={0} | all-to-all | bytes 131072 | tf_op jit(solution)/shard_map/cond/branch_1_fun/all_to_all | solution.py:182
  37.7 37.5 %all_to_all.24.refs_1_ = s16[16,208,128]{2,1,0:T(8,128)(2,1)S(1)} all-to-all(s16[16,208,128]{2,1,0:T(8,128)(2,1)} %get-tuple-element.54), channel_id=1, replica_groups=mesh['rep'=16,'fsdp'=8,'tp'=4] {'rep'}, dimensions={0} | all-to-all | bytes 1703936 | tf_op jit(solution)/shard_map/cond/branch_1_fun/all_to_all | solution.py:182
  75.2 0.8 swap.3
  76.0 0.0 copy-start.5
  76.0 0.0 copy-start.6
  76.1 0.0 copy-start.8
  76.1 0.0 copy-start.4
  76.1 43.6 %all_to_all.25.payload = s16[16,224,128]{2,1,0:T(8,128)(2,1)S(1)} all-to-all(s16[16,224,128]{2,1,0:T(8,128)(2,1)S(1)} %get-tuple-element.61), channel_id=1, replica_groups=mesh['rep'=16,'fsdp'=8,'tp'=4] {'rep'}, dimensions={0} | all-to-all | bytes 1835008 | tf_op jit(solution)/shard_map/all_to_all | solution.py:200
  119.7 0.0 copy-done.5
  119.7 0.0 copy-done.6
  119.7 0.0 copy-done.8
  119.7 0.0 copy-start
  119.8 0.0 copy-start.1
  119.8 0.0 copy-start.2
  119.8 0.0 copy-start.3
  119.8 0.0 copy-start.7
  119.8 0.5 squares.1
  120.3 12.9 %all_to_all.26.sums = f32[32,1,128]{2,1,0:T(1,128)S(1)} all-to-all(f32[32,1,128]{2,1,0:T(1,128)S(1)} %squares.1), channel_id=1, replica_groups=mesh['rep'=16,'fsdp'=8,'tp'=4] {'fsdp','tp'}, dimensions={0} | all-to-all | bytes 32768 | tf_op jit(solution)/shard_map/all_to_all | solution.py:209
  133.2 0.0 copy-done.4
  133.2 0.0 copy-done
  133.2 0.0 copy-done.1
  133.2 0.0 copy-done.2
  133.2 0.0 copy-done.3
  133.2 0.0 copy-done.7
  133.2 1.9 %update.1 = (f32[1,16,6400]{2,1,0:T(8,128)}, f32[1,16,6400]{2,1,0:T(8,128)}, f32[1,16,1280]{2,1,0:T(8,128)}, f32[1,16,6400]{2,1,0:T(8,128)}, f32[1,16,6400]{2,1,0:T(8,128)}, /*index=5*/f32[1,16,1280]{2,1,0:T(8,128)}) custom-call(f32[32,1,128]{2,1,0:T(1,128)S(1)} %all_to_all.26.sums, s16[16,224,128]{2,1,0:T(8,128)(2,1)S(1)} %all_to_all.25.payload, ...), custom_call_target="tpu_custom_call" | custom-call | tf_op jit(solution)/shard_map/update/pallas_call | solution.py:212
Async XLA Ops:
  0.6 0.7 copy-start.9
  76.0 43.7 %copy-start.5 = (bf16[1,16,6400]{2,1,0:T(8,128)(2,1)S(1)}, bf16[1,16,6400]{2,1,0:T(8,128)(2,1)}, u32[]{:S(2)}) copy-start(bf16[1,16,6400]{2,1,0:T(8,128)(2,1)} %gg.3) | copy-start | bytes 614404
  76.0 43.7 %copy-start.6 = (bf16[1,16,6400]{2,1,0:T(8,128)(2,1)S(1)}, bf16[1,16,6400]{2,1,0:T(8,128)(2,1)}, u32[]{:S(2)}) copy-start(bf16[1,16,6400]{2,1,0:T(8,128)(2,1)} %gu.3) | copy-start | bytes 614404
  76.1 43.7 %copy-start.8 = (bf16[1,16,1280]{2,1,0:T(8,128)(2,1)S(1)}, bf16[1,16,1280]{2,1,0:T(8,128)(2,1)}, u32[]{:S(2)}) copy-start(bf16[1,16,1280]{2,1,0:T(8,128)(2,1)} %gd.3) | copy-start | bytes 122884
  76.1 57.1 %copy-start.4 = (f32[1,16,6400]{2,1,0:T(8,128)S(1)}, f32[1,16,6400]{2,1,0:T(8,128)}, u32[]{:S(2)}) copy-start(f32[1,16,6400]{2,1,0:T(8,128)} %wu.1) | copy-start | bytes 1228804
  119.7 13.4 %copy-start = (f32[1,16,6400]{2,1,0:T(8,128)S(1)}, f32[1,16,6400]{2,1,0:T(8,128)}, u32[]{:S(2)}) copy-start(f32[1,16,6400]{2,1,0:T(8,128)} %mg.1) | copy-start | bytes 1228804
  119.8 13.4 %copy-start.1 = (f32[1,16,6400]{2,1,0:T(8,128)S(1)}, f32[1,16,6400]{2,1,0:T(8,128)}, u32[]{:S(2)}) copy-start(f32[1,16,6400]{2,1,0:T(8,128)} %mu.1) | copy-start | bytes 1228804
  119.8 13.4 %copy-start.2 = (f32[1,16,1280]{2,1,0:T(8,128)S(1)}, f32[1,16,1280]{2,1,0:T(8,128)}, u32[]{:S(2)}) copy-start(f32[1,16,1280]{2,1,0:T(8,128)} %md.1) | copy-start | bytes 245764
  119.8 13.4 %copy-start.3 = (f32[1,16,6400]{2,1,0:T(8,128)S(1)}, f32[1,16,6400]{2,1,0:T(8,128)}, u32[]{:S(2)}) copy-start(f32[1,16,6400]{2,1,0:T(8,128)} %wg.1) | copy-start | bytes 1228804
  119.8 13.4 %copy-start.7 = (f32[1,16,1280]{2,1,0:T(8,128)S(1)}, f32[1,16,1280]{2,1,0:T(8,128)}, u32[]{:S(2)}) copy-start(f32[1,16,1280]{2,1,0:T(8,128)} %wd.1) | copy-start | bytes 245764

commit v4 on v3

--- a/solution.py
+++ b/solution.py
@@ -16,6 +16,7 @@
 LANES = 128
 TOP = 32767.0
 STEPS = 16.0
+TINY = 2.0**-120
 VMEM_LIMIT = 24 * 1024 * 1024
 ENCODE_LIMIT = 60 * 1024 * 1024
 
@@ -40,7 +41,7 @@
 
 
 def exponent(peak):
-    power = jnp.ceil(STEPS * jnp.log2(jnp.maximum(peak, 2.0**-120)))
+    power = jnp.ceil(STEPS * jnp.log2(jnp.maximum(peak, TINY)))
     return jnp.clip(power, -120.0 * STEPS, 128.0 * STEPS - 1.0)
 
 
@@ -60,15 +61,15 @@
 
     def coded(block_ref, first):
         count = block_ref.shape[2] // LANES
-        peak = jnp.zeros((rows, LANES), jnp.float32)
-        for c in range(count):
-            peak = jnp.maximum(peak, jnp.abs(block_ref[0, :, c * LANES : (c + 1) * LANES].astype(jnp.float32)))
-        power = exponent(jnp.max(peak, axis=(0, 1), keepdims=True))
-        factor = jnp.broadcast_to(jnp.exp2(power * (-1.0 / STEPS)), (rows, LANES))
+        peak = jnp.abs(block_ref[0, :, 0:LANES])
+        for c in range(1, count):
+            peak = jnp.maximum(peak, jnp.abs(block_ref[0, :, c * LANES : (c + 1) * LANES]))
+        power = exponent(jnp.max(peak.astype(jnp.float32), axis=(0, 1), keepdims=True))
+        factor = jnp.broadcast_to(TOP * jnp.exp2(power * (-0.5 / STEPS)), (rows, LANES))
         for c in range(count):
             x = block_ref[0, :, c * LANES : (c + 1) * LANES].astype(jnp.float32)
-            level = jnp.minimum(TOP * jnp.sqrt(jnp.abs(x) * factor), TOP) + 0.5
-            level = jnp.where(x < 0, -level, level)
+            level = x * lax.rsqrt(jnp.maximum(jnp.abs(x), TINY)) * factor
+            level = jnp.clip(level, -TOP, TOP) + jnp.where(x < 0, -0.5, 0.5)
             put(first + c, level.astype(jnp.int32).astype(jnp.int16))
         return jnp.broadcast_to(power, (rows, LANES)).astype(jnp.int32)
 
@@ -83,8 +84,11 @@
         put(scales[slot], jnp.where(upper, power_w, power_g).astype(jnp.int16))
 
 
-def swap_kernel(starts, scales, cuts, rows, partner, me, *refs):
-    inps, out = refs[:-1], refs[-1]
+def swap_kernel(starts, scales, cuts, rows, partner_hbm, me, *refs):
+    inps, (out, partner, sem) = refs[: len(cuts)], refs[len(cuts) :]
+    fetch = pltpu.make_async_copy(partner_hbm, partner, sem)
+    fetch.start()
+    fetch.wait()
     replicas = out.shape[0]
     per_home = sum(cuts)
     for place in range(per_home):
@@ -131,7 +135,9 @@
     out[...] = jnp.broadcast_to(total[None], out.shape)
 
 
-def update_kernel(starts, scales, per_home, elements, sums, payload, wg, wu, wd, mg, mu, md, gg, gu, gd, og, ou, od, ng, nu, nd):
+def update_kernel(starts, scales, per_home, elements, sums, payload, wg, wu, wd, mg, mu, md, gg, gu, gd, *refs):
+    outs, (og, ou, od, ng, nu, nd), sems = refs[:6], refs[6:12], refs[12]
+    copies = [pltpu.make_async_copy(src, dst, sems.at[i]) for i, (src, dst) in enumerate(zip(refs[6:12], outs))]
     rows = gg.shape[1]
     get = reader(per_home, rows, payload)
     lane = lax.broadcasted_iota(jnp.int32, (1, LANES), 1)
@@ -152,6 +158,10 @@
             weight = w[0, :, part]
             n[0, :, part] = moment
             o[0, :, part] = weight - GAMMA * (weight - mate) - RATE * (scaled + BETA * moment)
+        copies[slot].start()
+        copies[3 + slot].start()
+    for copy in copies:
+        copy.wait()
 
 
 def local(partner, wg, wu, wd, mg, mu, md, gg, gu, gd):
@@ -185,14 +195,17 @@
         return pl.pallas_call(
             functools.partial(swap_kernel, starts, scales, cuts, rows),
             out_shape=packed,
-            in_specs=[smem, smem] + [vmem] * len(cuts),
+            in_specs=[pl.BlockSpec(memory_space=pl.ANY), smem] + [vmem] * len(cuts),
             out_specs=vmem,
+            scratch_shapes=[pltpu.SMEM(partner.shape, partner.dtype), pltpu.SemaphoreType.DMA],
             compiler_params=params,
             name="swap",
         )(operands[0], operands[1], *homed)
 
+    z_lo, core = jnp.divmod(lax.axis_index("fsdp"), 2)
+    inner = (z_lo == 1) | (z_lo == 2)
     swapped = lax.cond(
-        lax.rem(lax.axis_index("fsdp"), 2) == 1,
+        inner == (core == 0),
         functools.partial(outward, (1, per_home - 1)),
         functools.partial(outward, (per_home,)),
         partner, me, wg, wu, wd, gg, gu, gd,
@@ -213,7 +226,8 @@
         functools.partial(update_kernel, starts, scales, per_home, elements),
         out_shape=arrays,
         in_specs=[vmem] * 11,
-        out_specs=[vmem] * 6,
+        out_specs=[pl.BlockSpec(memory_space=pl.ANY)] * 6,
+        scratch_shapes=[pltpu.VMEM(a.shape, a.dtype) for a in arrays] + [pltpu.SemaphoreType.DMA((6,))],
         compiler_params=params,
         name="update",
     )(sums, mates, wg, wu, wd, mg, mu, md, gg, gu, gd)

time: 135 us -> 131 us (0.970)
  blocking collectives: 126 us -> 123 us
    all_to_all x1, blocking collectives: 12.9 us -> 24.1 us  [local(): sums = lax.all_to_all(partial, ('fsdp', 'tp'), 0, 0, tiled=True)]
    all_to_all x2, blocking collectives: 69.9 us -> 62.2 us  [outward(): homed.append(lax.all_to_all(coded[i], 'rep', 0, 0, tiled=True))]
    all_to_all x1, blocking collectives: 43.6 us -> 36.3 us  [local(): mates = lax.all_to_all(swapped, 'rep', 0, 0, tiled=True)]
where the time goes in v4:
time: 131 us
  blocking collectives  123 us (94%)
  Pallas kernels  6.39 us (5%)
    all_to_all x2, blocking collectives, outward(): homed.append(lax.all_to_all(coded[i], 'rep', 0, 0, tiled=True))  62.2 us
    all_to_all x1, blocking collectives, local(): mates = lax.all_to_all(swapped, 'rep', 0, 0, tiled=True)  36.3 us
    all_to_all x1, blocking collectives, local(): sums = lax.all_to_all(partial, ('fsdp', 'tp'), 0, 0, tiled=True)  24.1 us
    pallas_call x1, Pallas kernels, outward(): pl.pallas_call(functools.partial(encode_kernel, starts, scales, cuts), ou...  3.33 us

profile of v4, /device:TPU:1, one launch (start us, length us, event | category | flops | bytes accessed | tf_op | source)
XLA Modules:
  0.0 130.5 jit_solution(16459326782287017854)
XLA Ops:
  0.6 0.0 copy-start.8
  0.7 0.0 copy-start.9
  0.7 0.7 copy-done.8
  1.4 0.0 copy-done.9
  1.4 66.4 %conditional.1 = (s16[16,224,128]{2,1,0:T(8,128)(2,1)S(1)}) conditional(s32[]{:T(128)} %convert_element_type.3, (f32[1,16,6400]{2,1,0:T(8,128)}, f32[1,16,6400]{2,1,0:T(8,128)}, f32[1,16,1280]{2,1,0:T(8,128)}, bf16[1,16,6400]{2,1,0:T(8,128)(2,1)}, bf16[1,16,6400]{2,1,0:T(8,128)(2,1)}, /*index=5*/bf16[1,16,1280]{2,1,0:T(8,128)(2,1)S(1)}, ...), branch_computations={%region_0.1_spmd, %region_1.2_spmd} | conditional | bytes 1835016 | solution.py:207
  1.4 3.3 %encode.3 = (s16[16,16,128]{2,1,0:T(8,128)(2,1)}, s16[16,208,128]{2,1,0:T(8,128)(2,1)}) custom-call(f32[1,16,6400]{2,1,0:T(8,128)} %get-tuple-element.45.wg, f32[1,16,6400]{2,1,0:T(8,128)} %get-tuple-element.46.wu, f32[1,16,1280]{2,1,0:T(8,128)} %get-tuple-element.47.wd, bf16[1,16,6400]{2,1,0:T(8,128)(2,1)} %get-tuple-element.48.gg, ...), custom_call_target="tpu_custom_call" | custom-call | tf_op jit(solution)/shard_map/cond/branch_1_fun/encode/pallas_call | solution.py:180
  4.7 32.5 %all_to_all.23.refs_0_ = s16[16,16,128]{2,1,0:T(8,128)(2,1)S(1)} all-to-all(s16[16,16,128]{2,1,0:T(8,128)(2,1)} %get-tuple-element.51), channel_id=1, replica_groups=mesh['rep'=16,'fsdp'=8,'tp'=4] {'rep'}, dimensions={0} | all-to-all | bytes 131072 | tf_op jit(solution)/shard_map/cond/branch_1_fun/all_to_all | solution.py:192
  37.3 29.7 %all_to_all.24.refs_1_ = s16[16,208,128]{2,1,0:T(8,128)(2,1)S(1)} all-to-all(s16[16,208,128]{2,1,0:T(8,128)(2,1)} %get-tuple-element.54), channel_id=1, replica_groups=mesh['rep'=16,'fsdp'=8,'tp'=4] {'rep'}, dimensions={0} | all-to-all | bytes 1703936 | tf_op jit(solution)/shard_map/cond/branch_1_fun/all_to_all | solution.py:192
  67.0 0.8 swap.3
  67.8 0.0 copy-start.5
  67.8 0.0 copy-start.6
  67.8 0.0 copy-start.4
  67.9 36.3 %all_to_all.25.payload = s16[16,224,128]{2,1,0:T(8,128)(2,1)S(1)} all-to-all(s16[16,224,128]{2,1,0:T(8,128)(2,1)S(1)} %get-tuple-element.61), channel_id=1, replica_groups=mesh['rep'=16,'fsdp'=8,'tp'=4] {'rep'}, dimensions={0} | all-to-all | bytes 1835008 | tf_op jit(solution)/shard_map/all_to_all | solution.py:213
  104.1 0.0 copy-done.5
  104.1 0.0 copy-done.6
  104.2 0.0 copy-start
  104.2 0.0 copy-start.1
  104.2 0.0 copy-start.2
  104.2 0.0 copy-start.3
  104.2 0.0 copy-start.7
  104.2 0.5 squares.1
  104.7 24.1 %all_to_all.26.sums = f32[32,1,128]{2,1,0:T(1,128)S(1)} all-to-all(f32[32,1,128]{2,1,0:T(1,128)S(1)} %squares.1), channel_id=1, replica_groups=mesh['rep'=16,'fsdp'=8,'tp'=4] {'fsdp','tp'}, dimensions={0} | all-to-all | bytes 32768 | tf_op jit(solution)/shard_map/all_to_all | solution.py:222
  128.7 0.0 copy-done.4
  128.7 0.0 copy-done
  128.7 0.0 copy-done.1
  128.7 0.0 copy-done.2
  128.7 0.0 copy-done.3
  128.7 0.0 copy-done.7
  128.7 1.8 %update.1 = (f32[1,16,6400]{2,1,0:T(8,128)}, f32[1,16,6400]{2,1,0:T(8,128)}, f32[1,16,1280]{2,1,0:T(8,128)}, f32[1,16,6400]{2,1,0:T(8,128)}, f32[1,16,6400]{2,1,0:T(8,128)}, /*index=5*/f32[1,16,1280]{2,1,0:T(8,128)}) custom-call(f32[32,1,128]{2,1,0:T(1,128)S(1)} %all_to_all.26.sums, s16[16,224,128]{2,1,0:T(8,128)(2,1)S(1)} %all_to_all.25.payload, ...), custom_call_target="tpu_custom_call" | custom-call | tf_op jit(solution)/shard_map/update/pallas_call | solution.py:225
Async XLA Ops:
  0.6 0.8 copy-start.8
  0.7 0.7 copy-start.9
  67.8 36.3 %copy-start.5 = (bf16[1,16,6400]{2,1,0:T(8,128)(2,1)S(1)}, bf16[1,16,6400]{2,1,0:T(8,128)(2,1)}, u32[]{:S(2)}) copy-start(bf16[1,16,6400]{2,1,0:T(8,128)(2,1)} %gg.3) | copy-start | bytes 614404
  67.8 36.3 %copy-start.6 = (bf16[1,16,6400]{2,1,0:T(8,128)(2,1)S(1)}, bf16[1,16,6400]{2,1,0:T(8,128)(2,1)}, u32[]{:S(2)}) copy-start(bf16[1,16,6400]{2,1,0:T(8,128)(2,1)} %gu.3) | copy-start | bytes 614404
  67.8 60.9 %copy-start.4 = (f32[1,16,6400]{2,1,0:T(8,128)S(1)}, f32[1,16,6400]{2,1,0:T(8,128)}, u32[]{:S(2)}) copy-start(f32[1,16,6400]{2,1,0:T(8,128)} %wu.1) | copy-start | bytes 1228804
  104.2 24.6 %copy-start = (f32[1,16,6400]{2,1,0:T(8,128)S(1)}, f32[1,16,6400]{2,1,0:T(8,128)}, u32[]{:S(2)}) copy-start(f32[1,16,6400]{2,1,0:T(8,128)} %mg.1) | copy-start | bytes 1228804
  104.2 24.6 %copy-start.1 = (f32[1,16,6400]{2,1,0:T(8,128)S(1)}, f32[1,16,6400]{2,1,0:T(8,128)}, u32[]{:S(2)}) copy-start(f32[1,16,6400]{2,1,0:T(8,128)} %mu.1) | copy-start | bytes 1228804
  104.2 24.6 %copy-start.2 = (f32[1,16,1280]{2,1,0:T(8,128)S(1)}, f32[1,16,1280]{2,1,0:T(8,128)}, u32[]{:S(2)}) copy-start(f32[1,16,1280]{2,1,0:T(8,128)} %md.1) | copy-start | bytes 245764
  104.2 24.6 %copy-start.3 = (f32[1,16,6400]{2,1,0:T(8,128)S(1)}, f32[1,16,6400]{2,1,0:T(8,128)}, u32[]{:S(2)}) copy-start(f32[1,16,6400]{2,1,0:T(8,128)} %wg.1) | copy-start | bytes 1228804
  104.2 24.6 %copy-start.7 = (f32[1,16,1280]{2,1,0:T(8,128)S(1)}, f32[1,16,1280]{2,1,0:T(8,128)}, u32[]{:S(2)}) copy-start(f32[1,16,1280]{2,1,0:T(8,128)} %wd.1) | copy-start | bytes 245764

commit v5 on v4

v5 whole, which is shorter than its diff:
```python
import functools

import jax
import jax.numpy as jnp
from jax import lax
from jax.experimental import pallas as pl
from jax.experimental.pallas import tpu as pltpu
from jax.sharding import PartitionSpec as P

CLIP_RATIO = 0.5
BETA = 0.9
GAMMA = 0.4
RATE = 0.7
EPS = 1e-06

LANES = 128
TOP = 32767.0
STEPS = 16.0
TINY = 2.0**-120
VMEM_LIMIT = 24 * 1024 * 1024
ENCODE_LIMIT = 60 * 1024 * 1024


def plan(widths, replicas):
    counts = [width // LANES for width in widths]
    last = [(2, kind, c) for kind in range(2) for c in range(counts[2])]
    rest = [(slot, kind, c) for slot in range(2) for kind in range(2) for c in range(counts[slot])]
    rest += last[replicas:]
    bounds = (2 * counts[0], 2 * counts[0] + 2 * counts[1], len(rest))
    rest += [(slot, 2, 0) for slot in range(3)]
    more = -(-len(rest) // replicas)
    where = {tile: (i, 0) for i, tile in enumerate(last[:replicas])}
    where.update({tile: (i // more, 1 + i % more) for i, tile in enumerate(rest)})
    spare = [(i // more, 1 + i % more) for i in range(len(rest), more * replicas)]
    return where, spare, bounds, 1 + more


def exponent(peak):
    power = jnp.ceil(STEPS * jnp.log2(jnp.maximum(peak, TINY)))
    return jnp.clip(power, -120.0 * STEPS, 128.0 * STEPS - 1.0)


def encode_kernel(where, spare, first, count, names, *refs):
    n = len(names)
    srcs, out, dsts, sems = refs[:n], refs[n], refs[n + 1 : 2 * n + 1], refs[2 * n + 1]
    rows = srcs[0].shape[1]
    copies = [pltpu.make_async_copy(srcs[i], dsts[i], sems.at[i]) for i in range(n)]
    for copy in copies:
        copy.start()

    def put(at, value):
        home, place = at
        if first <= place < first + count:
            out[home, (place - first) * rows : (place - first + 1) * rows, :] = value

    for at in spare:
        put(at, jnp.zeros((rows, LANES), jnp.int16))
    powers = {}
    for (slot, kind), ref, copy in zip(names, dsts, copies):
        copy.wait()
        tiles = ref.shape[2] // LANES
        peak = jnp.abs(ref[0, :, 0:LANES])
        for c in range(1, tiles):
            peak = jnp.maximum(peak, jnp.abs(ref[0, :, c * LANES : (c + 1) * LANES]))
        power = exponent(jnp.max(peak.astype(jnp.float32), axis=(0, 1), keepdims=True))
        factor = jnp.broadcast_to(TOP * jnp.exp2(power * (-0.5 / STEPS)), (rows, LANES))
        for c in range(tiles):
            at = where[slot, kind, c]
            if first <= at[1] < first + count:
                x = ref[0, :, c * LANES : (c + 1) * LANES].astype(jnp.float32)
                level = x * lax.rsqrt(jnp.maximum(jnp.abs(x), TINY)) * factor
                level = jnp.round(jnp.clip(level, -TOP, TOP))
                put(at, level.astype(jnp.int32).astype(jnp.int16))
        powers[slot, kind] = jnp.broadcast_to(power, (rows, LANES)).astype(jnp.int32)
    if first + count > 1:
        upper = lax.broadcasted_iota(jnp.int32, (rows, LANES), 0) < 8
        for slot in range(3):
            put(where[slot, 2, 0], jnp.where(upper, powers[slot, 0], powers[slot, 1]).astype(jnp.int16))


def swap_kernel(bounds, cuts, rows, partner_hbm, me, *refs):
    inps, (out, partner, sem) = refs[: len(cuts)], refs[len(cuts) :]
    fetch = pltpu.make_async_copy(partner_hbm, partner, sem)
    fetch.start()
    fetch.wait()
    replicas = out.shape[0]
    more = sum(cuts) - 1
    for place in range(1 + more):
        slot = 2
        if place:
            tile = me[0] * more + place - 1
            slot = jnp.where(tile < bounds[0], 0, jnp.where(tile < bounds[1], 1, 2))
            slot = jnp.where(tile == bounds[2], 0, jnp.where(tile == bounds[2] + 1, 1, slot))
        inp, at = locate(inps, cuts, place)
        for r in range(replicas):
            source = partner[slot, r]
            out[r, place * rows : (place + 1) * rows, :] = inp[source, at * rows : (at + 1) * rows, :]


def locate(parts, cuts, place):
    for part, cut in zip(parts, cuts):
        if place < cut:
            return part, place
        place -= cut
    raise ValueError("place")


def reader(where, rows, payload):
    def get(*tile):
        home, place = where[tile]
        return payload[home, place * rows : (place + 1) * rows, :].astype(jnp.int32).astype(jnp.float32)

    return get


def decoded(code, scale):
    a = code * (1.0 / TOP)
    return a * jnp.abs(a) * scale


def scales_of(get, slot):
    power = jnp.exp2(get(slot, 2, 0) * (1.0 / STEPS))
    return power[0:1, :], power[8:9, :]


def squares_kernel(where, payload, gg, gu, gd, out):
    rows = gg.shape[1]
    get = reader(where, rows, payload)
    lane = lax.broadcasted_iota(jnp.int32, (1, LANES), 1)
    total = jnp.zeros((1, LANES), jnp.float32)
    for slot, g in enumerate((gg, gu, gd)):
        _, scale = scales_of(get, slot)
        sums = jnp.zeros((rows, LANES), jnp.float32)
        for c in range(g.shape[2] // LANES):
            own = g[0, :, c * LANES : (c + 1) * LANES].astype(jnp.float32)
            mixed = 0.5 * (own + decoded(get(slot, 1, c), scale))
            sums = sums + mixed * mixed
        total = jnp.where(lane == slot, jnp.sum(sums, axis=(0, 1), keepdims=True), total)
    out[...] = jnp.broadcast_to(total[None], out.shape)


def update_kernel(where, elements, sums, payload, wg, wu, wd, mg, mu, md, gg, gu, gd, *refs):
    outs, (og, ou, od, ng, nu, nd), sems = refs[:6], refs[6:12], refs[12]
    copies = [pltpu.make_async_copy(src, dst, sems.at[i]) for i, (src, dst) in enumerate(zip(refs[6:12], outs))]
    rows = gg.shape[1]
    get = reader(where, rows, payload)
    lane = lax.broadcasted_iota(jnp.int32, (1, LANES), 1)
    totals = jnp.sum(sums[...], axis=0)
    groups = ((wg, mg, gg, og, ng), (wu, mu, gu, ou, nu), (wd, md, gd, od, nd))
    for slot, (w, m, g, o, n) in enumerate(groups):
        scale_w, scale_g = scales_of(get, slot)
        squares = jnp.sum(jnp.where(lane == slot, totals, 0.0), axis=(0, 1), keepdims=True)
        bound = CLIP_RATIO * float(elements[slot]) ** 0.5
        clip = jnp.broadcast_to(jnp.minimum(1.0, bound / jnp.sqrt(squares + EPS)), (rows, LANES))
        for c in range(w.shape[2] // LANES):
            part = slice(c * LANES, (c + 1) * LANES)
            own = g[0, :, part].astype(jnp.float32)
            mixed = 0.5 * (own + decoded(get(slot, 1, c), scale_g))
            mate = decoded(get(slot, 0, c), scale_w)
            scaled = clip * mixed
            moment = BETA * m[0, :, part] + scaled
            weight = w[0, :, part]
            n[0, :, part] = moment
            o[0, :, part] = weight - GAMMA * (weight - mate) - RATE * (scaled + BETA * moment)
        copies[slot].start()
        copies[3 + slot].start()
    for copy in copies:
        copy.wait()


def local(partner, wg, wu, wd, mg, mu, md, gg, gu, gd):
    replicas = lax.axis_size("rep")
    shards = lax.axis_size("fsdp") * lax.axis_size("tp")
    rows = wg.shape[1]
    where, spare, bounds, per_home = plan((wg.shape[2], wu.shape[2], wd.shape[2]), replicas)
    params = pltpu.CompilerParams(vmem_limit_bytes=VMEM_LIMIT)
    vmem = pl.BlockSpec(memory_space=pltpu.VMEM)
    smem = pl.BlockSpec(memory_space=pltpu.SMEM)
    packed = jax.ShapeDtypeStruct((replicas, per_home * rows, LANES), jnp.int16)

    me = lax.axis_index("rep").reshape(1).astype(jnp.int32)

    def encode(arrays, first, count):
        return pl.pallas_call(
            functools.partial(encode_kernel, where, spare, first, count, tuple(arrays)),
            out_shape=jax.ShapeDtypeStruct((replicas, count * rows, LANES), jnp.int16),
            in_specs=[pl.BlockSpec(memory_space=pl.ANY)] * len(arrays),
            out_specs=vmem,
            scratch_shapes=[pltpu.VMEM(a.shape, a.dtype) for a in arrays.values()]
            + [pltpu.SemaphoreType.DMA((len(arrays),))],
            compiler_params=pltpu.CompilerParams(vmem_limit_bytes=ENCODE_LIMIT),
            name="encode",
        )(*arrays.values())

    def swap(partner, me, cuts, homed):
        return pl.pallas_call(
            functools.partial(swap_kernel, bounds, cuts, rows),
            out_shape=packed,
            in_specs=[pl.BlockSpec(memory_space=pl.ANY), smem] + [vmem] * len(cuts),
            out_specs=vmem,
            scratch_shapes=[pltpu.SMEM(partner.shape, partner.dtype), pltpu.SemaphoreType.DMA],
            compiler_params=params,
            name="swap",
        )(partner, me, *homed)

    def named(wg, wu, wd, gg, gu, gd):
        return {(2, 0): wd, (2, 1): gd, (0, 0): wg, (0, 1): gg, (1, 0): wu, (1, 1): gu}

    def early(partner, me, *arrays):
        coded = encode(named(*arrays), 0, per_home)
        return swap(partner, me, (per_home,), (lax.all_to_all(coded, "rep", 0, 0, tiled=True),))

    def late(partner, me, *arrays):
        named_arrays = named(*arrays)
        down = {key: a for key, a in named_arrays.items() if key[0] == 2}
        head = lax.all_to_all(encode(down, 0, 1), "rep", 0, 0, tiled=True)
        coded = encode(named_arrays, 1, per_home - 1)
        head, coded = lax.optimization_barrier((head, coded))
        tail = lax.all_to_all(coded, "rep", 0, 0, tiled=True)
        return swap(partner, me, (1, per_home - 1), (head, tail))

    z_lo, core = jnp.divmod(lax.axis_index("fsdp"), 2)
    swapped = lax.cond(
        lax.rem(z_lo + core, 2) == 0,
        late,
        early,
        partner, me, wg, wu, wd, gg, gu, gd,
    )
    mates = lax.all_to_all(swapped, "rep", 0, 0, tiled=True)
    partial = pl.pallas_call(
        functools.partial(squares_kernel, where),
        out_shape=jax.ShapeDtypeStruct((shards, 1, LANES), jnp.float32),
        in_specs=[vmem] * 4,
        out_specs=vmem,
        compiler_params=params,
        name="squares",
    )(mates, gg, gu, gd)
    sums = lax.all_to_all(partial, ("fsdp", "tp"), 0, 0, tiled=True)
    elements = tuple(shards * w.shape[1] * w.shape[2] for w in (wg, wu, wd))
    arrays = [jax.ShapeDtypeStruct(a.shape, jnp.float32) for a in (wg, wu, wd, mg, mu, md)]
    return pl.pallas_call(
        functools.partial(update_kernel, where, elements),
        out_shape=arrays,
        in_specs=[vmem] * 11,
        out_specs=[pl.BlockSpec(memory_space=pl.ANY)] * 6,
        scratch_shapes=[pltpu.VMEM(a.shape, a.dtype) for a in arrays] + [pltpu.SemaphoreType.DMA((6,))],
        compiler_params=params,
        name="update",
    )(sums, mates, wg, wu, wd, mg, mu, md, gg, gu, gd)


def solution(mesh):
    spec = P("rep", "fsdp", "tp")
    return jax.shard_map(
        local,
        mesh=mesh,
        in_specs=(P(),) + (spec,) * 9,
        out_specs=(spec,) * 6,
        check_vma=False,
    )
```

time: 131 us -> 130 us (level)
    all_to_all x1, blocking collectives: 24.1 us -> 44.5 us  [local(): sums = lax.all_to_all(partial, ('fsdp', 'tp'), 0, 0, tiled=True)]
    all_to_all x2 -> x1, blocking collectives: 62.2 us -> 46.7 us  [early(): lax.all_to_all(coded, 'rep', 0, 0, tiled=True)]
    all_to_all x1, blocking collectives: 36.3 us -> 30.4 us  [local(): mates = lax.all_to_all(swapped, 'rep', 0, 0, tiled=True)]
where the time goes in v5:
time: 130 us; the launch traced here: 129 us
  blocking collectives  122 us (94%)
  Pallas kernels  6.19 us (5%)
    all_to_all x1, blocking collectives, early(): lax.all_to_all(coded, 'rep', 0, 0, tiled=True)  46.7 us
    all_to_all x1, blocking collectives, local(): sums = lax.all_to_all(partial, ('fsdp', 'tp'), 0, 0, tiled=True)  44.5 us
    all_to_all x1, blocking collectives, local(): mates = lax.all_to_all(swapped, 'rep', 0, 0, tiled=True)  30.4 us
    pallas_call x1, Pallas kernels, encode(): pl.pallas_call(functools.partial(encode_kernel, where, spare, first, coun...  3.13 us

profile of v5, /device:TPU:1, one launch (start us, length us, event | category | flops | bytes accessed | tf_op | source)
XLA Modules:
  0.0 129.4 jit_solution(14960721768596856932)
XLA Ops:
  0.6 0.0 copy-start.10
  0.7 0.0 copy-start.11
  0.7 0.7 copy-done.10
  1.4 0.0 copy-done.11
  1.4 50.7 %conditional.1 = (s16[16,224,128]{2,1,0:T(8,128)(2,1)S(1)}) conditional(s32[]{:T(128)} %convert_element_type.3, (f32[1,16,1280]{2,1,0:T(8,128)}, bf16[1,16,1280]{2,1,0:T(8,128)(2,1)S(1)}, f32[1,16,6400]{2,1,0:T(8,128)}, bf16[1,16,6400]{2,1,0:T(8,128)(2,1)}, f32[1,16,6400]{2,1,0:T(8,128)}, /*index=5*/bf16[1,16,6400]{2,1,0:T(8,128)(2,1)}, ...), branch_computations={%region_0.1_spmd, %region_1.2_spmd} | conditional | bytes 3047520 | solution.py:223
  1.4 3.1 %encode.3 = s16[16,224,128]{2,1,0:T(8,128)(2,1)} custom-call(f32[1,16,1280]{2,1,0:T(8,128)} %get-tuple-element.37.refs_0_, bf16[1,16,1280]{2,1,0:T(8,128)(2,1)S(1)} %get-tuple-element.38.refs_1_, f32[1,16,6400]{2,1,0:T(8,128)} %get-tuple-element.39.refs_2_, bf16[1,16,6400]{2,1,0:T(8,128)(2,1)} %get-tuple-element.40.refs_3_, ...), custom_call_target="tpu_custom_call" | custom-call | tf_op jit(solution)/shard_map/cond/branch_0_fun/encode/pallas_call | solution.py:184
  4.6 46.7 %all_to_all.22.refs_0_ = s16[16,224,128]{2,1,0:T(8,128)(2,1)S(1)} all-to-all(s16[16,224,128]{2,1,0:T(8,128)(2,1)} %encode.3), channel_id=1, replica_groups=mesh['rep'=16,'fsdp'=8,'tp'=4] {'rep'}, dimensions={0} | all-to-all | bytes 1835008 | tf_op jit(solution)/shard_map/cond/branch_0_fun/all_to_all | solution.py:211
  51.3 0.8 swap.2
  52.1 0.0 copy-start.5
  52.1 0.0 copy-start.7
  52.1 0.0 copy-start.4
  52.1 30.4 %all_to_all.24.payload = s16[16,224,128]{2,1,0:T(8,128)(2,1)S(1)} all-to-all(s16[16,224,128]{2,1,0:T(8,128)(2,1)S(1)} %get-tuple-element.59), channel_id=1, replica_groups=mesh['rep'=16,'fsdp'=8,'tp'=4] {'rep'}, dimensions={0} | all-to-all | bytes 1835008 | tf_op jit(solution)/shard_map/all_to_all | solution.py:229
  82.6 0.0 copy-done.5
  82.6 0.0 copy-done.7
  82.6 0.0 copy-start
  82.6 0.0 copy-start.1
  82.6 0.0 copy-start.2
  82.6 0.0 copy-start.3
  82.6 0.0 copy-start.8
  82.6 0.5 squares.1
  83.1 44.5 %all_to_all.25.sums = f32[32,1,128]{2,1,0:T(1,128)S(1)} all-to-all(f32[32,1,128]{2,1,0:T(1,128)S(1)} %squares.1), channel_id=1, replica_groups=mesh['rep'=16,'fsdp'=8,'tp'=4] {'fsdp','tp'}, dimensions={0} | all-to-all | bytes 32768 | tf_op jit(solution)/shard_map/all_to_all | solution.py:238
  127.6 0.0 copy-done.4
  127.6 0.0 copy-done
  127.6 0.0 copy-done.1
  127.6 0.0 copy-done.2
  127.6 0.0 copy-done.3
  127.6 0.0 copy-done.8
  127.6 1.8 %update.1 = (f32[1,16,6400]{2,1,0:T(8,128)}, f32[1,16,6400]{2,1,0:T(8,128)}, f32[1,16,1280]{2,1,0:T(8,128)}, f32[1,16,6400]{2,1,0:T(8,128)}, f32[1,16,6400]{2,1,0:T(8,128)}, /*index=5*/f32[1,16,1280]{2,1,0:T(8,128)}) custom-call(f32[32,1,128]{2,1,0:T(1,128)S(1)} %all_to_all.25.sums, s16[16,224,128]{2,1,0:T(8,128)(2,1)S(1)} %all_to_all.24.payload, ...), custom_call_target="tpu_custom_call" | custom-call | tf_op jit(solution)/shard_map/update/pallas_call | solution.py:241
Async XLA Ops:
  0.6 0.8 copy-start.10
  0.7 0.7 copy-start.11
  52.1 30.4 %copy-start.5 = (bf16[1,16,6400]{2,1,0:T(8,128)(2,1)S(1)}, bf16[1,16,6400]{2,1,0:T(8,128)(2,1)}, u32[]{:S(2)}) copy-start(bf16[1,16,6400]{2,1,0:T(8,128)(2,1)} %gg.3) | copy-start | bytes 614404
  52.1 30.4 %copy-start.7 = (bf16[1,16,6400]{2,1,0:T(8,128)(2,1)S(1)}, bf16[1,16,6400]{2,1,0:T(8,128)(2,1)}, u32[]{:S(2)}) copy-start(bf16[1,16,6400]{2,1,0:T(8,128)(2,1)} %gu.3) | copy-start | bytes 614404
  52.1 75.4 %copy-start.4 = (f32[1,16,6400]{2,1,0:T(8,128)S(1)}, f32[1,16,6400]{2,1,0:T(8,128)}, u32[]{:S(2)}) copy-start(f32[1,16,6400]{2,1,0:T(8,128)} %wu.1) | copy-start | bytes 1228804
  82.6 45.0 %copy-start = (f32[1,16,6400]{2,1,0:T(8,128)S(1)}, f32[1,16,6400]{2,1,0:T(8,128)}, u32[]{:S(2)}) copy-start(f32[1,16,6400]{2,1,0:T(8,128)} %mg.1) | copy-start | bytes 1228804
  82.6 45.0 %copy-start.1 = (f32[1,16,6400]{2,1,0:T(8,128)S(1)}, f32[1,16,6400]{2,1,0:T(8,128)}, u32[]{:S(2)}) copy-start(f32[1,16,6400]{2,1,0:T(8,128)} %mu.1) | copy-start | bytes 1228804
  82.6 45.0 %copy-start.2 = (f32[1,16,1280]{2,1,0:T(8,128)S(1)}, f32[1,16,1280]{2,1,0:T(8,128)}, u32[]{:S(2)}) copy-start(f32[1,16,1280]{2,1,0:T(8,128)} %md.1) | copy-start | bytes 245764
  82.6 45.0 %copy-start.3 = (f32[1,16,6400]{2,1,0:T(8,128)S(1)}, f32[1,16,6400]{2,1,0:T(8,128)}, u32[]{:S(2)}) copy-start(f32[1,16,6400]{2,1,0:T(8,128)} %wg.1) | copy-start | bytes 1228804
  82.6 45.0 %copy-start.8 = (f32[1,16,1280]{2,1,0:T(8,128)S(1)}, f32[1,16,1280]{2,1,0:T(8,128)}, u32[]{:S(2)}) copy-start(f32[1,16,1280]{2,1,0:T(8,128)} %wd.1) | copy-start | bytes 245764

commit v6 on v5

--- a/solution.py
+++ b/solution.py
@@ -17,6 +17,8 @@
 TOP = 32767.0
 STEPS = 16.0
 TINY = 2.0**-120
+REPLICAS = 16
+ORDER = 11
 VMEM_LIMIT = 24 * 1024 * 1024
 ENCODE_LIMIT = 60 * 1024 * 1024
 
@@ -35,12 +37,20 @@
     return where, spare, bounds, 1 + more
 
 
+def place_of(order, index):
+    return (order + REPLICAS - index) % REPLICAS
+
+
+def groups_of(order):
+    return [[place_of(order, i) for i in range(REPLICAS)]]
+
+
 def exponent(peak):
     power = jnp.ceil(STEPS * jnp.log2(jnp.maximum(peak, TINY)))
     return jnp.clip(power, -120.0 * STEPS, 128.0 * STEPS - 1.0)
 
 
-def encode_kernel(where, spare, first, count, names, *refs):
+def encode_kernel(where, spare, first, count, order, names, *refs):
     n = len(names)
     srcs, out, dsts, sems = refs[:n], refs[n], refs[n + 1 : 2 * n + 1], refs[2 * n + 1]
     rows = srcs[0].shape[1]
@@ -51,7 +61,7 @@
     def put(at, value):
         home, place = at
         if first <= place < first + count:
-            out[home, (place - first) * rows : (place - first + 1) * rows, :] = value
+            out[place_of(order, home), (place - first) * rows : (place - first + 1) * rows, :] = value
 
     for at in spare:
         put(at, jnp.zeros((rows, LANES), jnp.int16))
@@ -78,7 +88,7 @@
             put(where[slot, 2, 0], jnp.where(upper, powers[slot, 0], powers[slot, 1]).astype(jnp.int16))
 
 
-def swap_kernel(bounds, cuts, rows, partner_hbm, me, *refs):
+def swap_kernel(bounds, cuts, rows, order, partner_hbm, me, *refs):
     inps, (out, partner, sem) = refs[: len(cuts)], refs[len(cuts) :]
     fetch = pltpu.make_async_copy(partner_hbm, partner, sem)
     fetch.start()
@@ -93,8 +103,8 @@
             slot = jnp.where(tile == bounds[2], 0, jnp.where(tile == bounds[2] + 1, 1, slot))
         inp, at = locate(inps, cuts, place)
         for r in range(replicas):
-            source = partner[slot, r]
-            out[r, place * rows : (place + 1) * rows, :] = inp[source, at * rows : (at + 1) * rows, :]
+            source = place_of(order, partner[slot, r])
+            out[place_of(ORDER, r), place * rows : (place + 1) * rows, :] = inp[source, at * rows : (at + 1) * rows, :]
 
 
 def locate(parts, cuts, place):
@@ -108,7 +118,7 @@
 def reader(where, rows, payload):
     def get(*tile):
         home, place = where[tile]
-        return payload[home, place * rows : (place + 1) * rows, :].astype(jnp.int32).astype(jnp.float32)
+        return payload[place_of(ORDER, home), place * rows : (place + 1) * rows, :].astype(jnp.int32).astype(jnp.float32)
 
     return get
 
@@ -180,9 +190,9 @@
 
     me = lax.axis_index("rep").reshape(1).astype(jnp.int32)
 
-    def encode(arrays, first, count):
+    def encode(arrays, first, count, order):
         return pl.pallas_call(
-            functools.partial(encode_kernel, where, spare, first, count, tuple(arrays)),
+            functools.partial(encode_kernel, where, spare, first, count, order, tuple(arrays)),
             out_shape=jax.ShapeDtypeStruct((replicas, count * rows, LANES), jnp.int16),
             in_specs=[pl.BlockSpec(memory_space=pl.ANY)] * len(arrays),
             out_specs=vmem,
@@ -192,9 +202,9 @@
             name="encode",
         )(*arrays.values())
 
-    def swap(partner, me, cuts, homed):
+    def swap(partner, me, cuts, order, homed):
         return pl.pallas_call(
-            functools.partial(swap_kernel, bounds, cuts, rows),
+            functools.partial(swap_kernel, bounds, cuts, rows, order),
             out_shape=packed,
             in_specs=[pl.BlockSpec(memory_space=pl.ANY), smem] + [vmem] * len(cuts),
             out_specs=vmem,
@@ -206,18 +216,21 @@
     def named(wg, wu, wd, gg, gu, gd):
         return {(2, 0): wd, (2, 1): gd, (0, 0): wg, (0, 1): gg, (1, 0): wu, (1, 1): gu}
 
+    def send(payload, order):
+        return lax.all_to_all(payload, "rep", 0, 0, tiled=True, axis_index_groups=groups_of(order))
+
     def early(partner, me, *arrays):
-        coded = encode(named(*arrays), 0, per_home)
-        return swap(partner, me, (per_home,), (lax.all_to_all(coded, "rep", 0, 0, tiled=True),))
+        coded = encode(named(*arrays), 0, per_home, ORDER)
+        return swap(partner, me, (per_home,), ORDER, (send(coded, ORDER),))
 
     def late(partner, me, *arrays):
         named_arrays = named(*arrays)
         down = {key: a for key, a in named_arrays.items() if key[0] == 2}
-        head = lax.all_to_all(encode(down, 0, 1), "rep", 0, 0, tiled=True)
-        coded = encode(named_arrays, 1, per_home - 1)
+        head = send(encode(down, 0, 1, ORDER), ORDER)
+        coded = encode(named_arrays, 1, per_home - 1, ORDER)
         head, coded = lax.optimization_barrier((head, coded))
-        tail = lax.all_to_all(coded, "rep", 0, 0, tiled=True)
-        return swap(partner, me, (1, per_home - 1), (head, tail))
+        tail = send(coded, ORDER)
+        return swap(partner, me, (1, per_home - 1), ORDER, (head, tail))
 
     z_lo, core = jnp.divmod(lax.axis_index("fsdp"), 2)
     swapped = lax.cond(
@@ -226,7 +239,7 @@
         early,
         partner, me, wg, wu, wd, gg, gu, gd,
     )
-    mates = lax.all_to_all(swapped, "rep", 0, 0, tiled=True)
+    mates = send(swapped, ORDER)
     partial = pl.pallas_call(
         functools.partial(squares_kernel, where),
         out_shape=jax.ShapeDtypeStruct((shards, 1, LANES), jnp.float32),

time: 130 us -> 125 us (0.962)
  blocking collectives: 122 us -> 117 us
    all_to_all x1, blocking collectives: 44.5 us -> 22.8 us  [local(): sums = lax.all_to_all(partial, ('fsdp', 'tp'), 0, 0, tiled=True)]
    all_to_all x2, blocking collectives: 77.1 us -> 93.9 us  [send(): lax.all_to_all(payload, 'rep', 0, 0, tiled=True, axis_index_groups=groups...]
where the time goes in v6:
time: 125 us
  blocking collectives  117 us (94%)
  Pallas kernels  6.78 us (5%)
    all_to_all x2, blocking collectives, send(): lax.all_to_all(payload, 'rep', 0, 0, tiled=True, axis_index_groups=groups...  93.9 us
    all_to_all x1, blocking collectives, local(): sums = lax.all_to_all(partial, ('fsdp', 'tp'), 0, 0, tiled=True)  22.8 us
    pallas_call x1, Pallas kernels, encode(): pl.pallas_call(functools.partial(encode_kernel, where, spare, first, coun...  3.13 us

profile of v6, /device:TPU:1, one launch (start us, length us, event | category | flops | bytes accessed | tf_op | source)
XLA Modules:
  0.0 125.0 jit_solution(694427922573100808)
XLA Ops:
  0.6 0.0 copy-start.10
  0.7 0.0 copy-start.11
  0.7 0.7 copy-done.10
  1.4 0.0 copy-done.11
  1.4 51.6 %conditional.1 = (s16[16,224,128]{2,1,0:T(8,128)(2,1)S(1)}) conditional(s32[]{:T(128)} %convert_element_type.3, (f32[1,16,1280]{2,1,0:T(8,128)}, bf16[1,16,1280]{2,1,0:T(8,128)(2,1)S(1)}, f32[1,16,6400]{2,1,0:T(8,128)}, bf16[1,16,6400]{2,1,0:T(8,128)(2,1)}, f32[1,16,6400]{2,1,0:T(8,128)}, /*index=5*/bf16[1,16,6400]{2,1,0:T(8,128)(2,1)}, ...), branch_computations={%region_0.1_spmd, %region_1.2_spmd} | conditional | bytes 3047520 | solution.py:236
  1.4 3.1 %encode.3 = s16[16,224,128]{2,1,0:T(8,128)(2,1)} custom-call(f32[1,16,1280]{2,1,0:T(8,128)} %get-tuple-element.37.refs_0_, bf16[1,16,1280]{2,1,0:T(8,128)(2,1)S(1)} %get-tuple-element.38.refs_1_, f32[1,16,6400]{2,1,0:T(8,128)} %get-tuple-element.39.refs_2_, bf16[1,16,6400]{2,1,0:T(8,128)(2,1)} %get-tuple-element.40.refs_3_, ...), custom_call_target="tpu_custom_call" | custom-call | tf_op jit(solution)/shard_map/cond/branch_0_fun/encode/pallas_call | solution.py:194
  4.6 47.1 %all_to_all.22.refs_0_ = s16[16,224,128]{2,1,0:T(8,128)(2,1)S(1)} all-to-all(s16[16,224,128]{2,1,0:T(8,128)(2,1)} %encode.3), channel_id=1, replica_groups={{352,320,288,256,224,192,160,128,96,64,32,0,480,448,416,384},{353,321,2..., dimensions={0} | all-to-all | bytes 1835008 | tf_op jit(solution)/shard_map/cond/branch_0_fun/all_to_all | solution.py:220
  51.6 1.4 %swap.2 = s16[16,224,128]{2,1,0:T(8,128)(2,1)S(1)} custom-call(s32[3,16]{1,0:T(4,128)S(1)} %get-tuple-element.23.partner_hbm, s32[1]{0:T(128)} %get-tuple-element.36.me, s16[16,224,128]{2,1,0:T(8,128)(2,1)S(1)} %all_to_all.22.refs_0_), custom_call_target="tpu_custom_call" | custom-call | tf_op jit(solution)/shard_map/cond/branch_0_fun/swap/pallas_call | solution.py:206
  53.1 0.0 copy-start.5
  53.1 0.0 copy-start.7
  53.1 0.0 copy-start.4
  53.1 46.8 %all_to_all.24.payload = s16[16,224,128]{2,1,0:T(8,128)(2,1)S(1)} all-to-all(s16[16,224,128]{2,1,0:T(8,128)(2,1)S(1)} %get-tuple-element.59), channel_id=1, replica_groups={{352,320,288,256,224,192,160,128,96,64,32,0,480,448,416,384},{353,321,2..., dimensions={0} | all-to-all | bytes 1835008 | tf_op jit(solution)/shard_map/all_to_all | solution.py:220
  99.9 0.0 copy-done.5
  99.9 0.0 copy-done.7
  99.9 0.0 copy-start
  99.9 0.0 copy-start.1
  99.9 0.0 copy-start.2
  99.9 0.0 copy-start.3
  99.9 0.0 copy-start.8
  100.0 0.5 squares.1
  100.4 22.8 %all_to_all.25.sums = f32[32,1,128]{2,1,0:T(1,128)S(1)} all-to-all(f32[32,1,128]{2,1,0:T(1,128)S(1)} %squares.1), channel_id=1, replica_groups=mesh['rep'=16,'fsdp'=8,'tp'=4] {'fsdp','tp'}, dimensions={0} | all-to-all | bytes 32768 | tf_op jit(solution)/shard_map/all_to_all | solution.py:251
  123.2 0.0 copy-done.4
  123.2 0.0 copy-done
  123.2 0.0 copy-done.1
  123.2 0.0 copy-done.2
  123.2 0.0 copy-done.3
  123.2 0.0 copy-done.8
  123.2 1.8 %update.1 = (f32[1,16,6400]{2,1,0:T(8,128)}, f32[1,16,6400]{2,1,0:T(8,128)}, f32[1,16,1280]{2,1,0:T(8,128)}, f32[1,16,6400]{2,1,0:T(8,128)}, f32[1,16,6400]{2,1,0:T(8,128)}, /*index=5*/f32[1,16,1280]{2,1,0:T(8,128)}) custom-call(f32[32,1,128]{2,1,0:T(1,128)S(1)} %all_to_all.25.sums, s16[16,224,128]{2,1,0:T(8,128)(2,1)S(1)} %all_to_all.24.payload, ...), custom_call_target="tpu_custom_call" | custom-call | tf_op jit(solution)/shard_map/update/pallas_call | solution.py:254
Async XLA Ops:
  0.6 0.8 copy-start.10
  0.7 0.7 copy-start.11
  53.1 46.9 %copy-start.5 = (bf16[1,16,6400]{2,1,0:T(8,128)(2,1)S(1)}, bf16[1,16,6400]{2,1,0:T(8,128)(2,1)}, u32[]{:S(2)}) copy-start(bf16[1,16,6400]{2,1,0:T(8,128)(2,1)} %gg.3) | copy-start | bytes 614404
  53.1 46.8 %copy-start.7 = (bf16[1,16,6400]{2,1,0:T(8,128)(2,1)S(1)}, bf16[1,16,6400]{2,1,0:T(8,128)(2,1)}, u32[]{:S(2)}) copy-start(bf16[1,16,6400]{2,1,0:T(8,128)(2,1)} %gu.3) | copy-start | bytes 614404
  53.1 70.1 %copy-start.4 = (f32[1,16,6400]{2,1,0:T(8,128)S(1)}, f32[1,16,6400]{2,1,0:T(8,128)}, u32[]{:S(2)}) copy-start(f32[1,16,6400]{2,1,0:T(8,128)} %wu.1) | copy-start | bytes 1228804
  99.9 23.3 %copy-start = (f32[1,16,6400]{2,1,0:T(8,128)S(1)}, f32[1,16,6400]{2,1,0:T(8,128)}, u32[]{:S(2)}) copy-start(f32[1,16,6400]{2,1,0:T(8,128)} %mg.1) | copy-start | bytes 1228804
  99.9 23.3 %copy-start.1 = (f32[1,16,6400]{2,1,0:T(8,128)S(1)}, f32[1,16,6400]{2,1,0:T(8,128)}, u32[]{:S(2)}) copy-start(f32[1,16,6400]{2,1,0:T(8,128)} %mu.1) | copy-start | bytes 1228804
  99.9 23.3 %copy-start.2 = (f32[1,16,1280]{2,1,0:T(8,128)S(1)}, f32[1,16,1280]{2,1,0:T(8,128)}, u32[]{:S(2)}) copy-start(f32[1,16,1280]{2,1,0:T(8,128)} %md.1) | copy-start | bytes 245764
  99.9 23.3 %copy-start.3 = (f32[1,16,6400]{2,1,0:T(8,128)S(1)}, f32[1,16,6400]{2,1,0:T(8,128)}, u32[]{:S(2)}) copy-start(f32[1,16,6400]{2,1,0:T(8,128)} %wg.1) | copy-start | bytes 1228804
  99.9 23.3 %copy-start.8 = (f32[1,16,1280]{2,1,0:T(8,128)S(1)}, f32[1,16,1280]{2,1,0:T(8,128)}, u32[]{:S(2)}) copy-start(f32[1,16,1280]{2,1,0:T(8,128)} %wd.1) | copy-start | bytes 245764

commit v7 on v6

--- a/solution.py
+++ b/solution.py
@@ -18,7 +18,7 @@
 STEPS = 16.0
 TINY = 2.0**-120
 REPLICAS = 16
-ORDER = 11
+ORDER = 10
 VMEM_LIMIT = 24 * 1024 * 1024
 ENCODE_LIMIT = 60 * 1024 * 1024
 

time: 125 us -> 124 us (level)
  blocking collectives: 117 us -> 115 us
    all_to_all x1, blocking collectives: 22.8 us -> 20.8 us  [local(): sums = lax.all_to_all(partial, ('fsdp', 'tp'), 0, 0, tiled=True)]
where the time goes in v7:
time: 124 us; the launch traced here: 123 us
  blocking collectives  115 us (93%)
  Pallas kernels  6.78 us (5%)
    all_to_all x2, blocking collectives, send(): lax.all_to_all(payload, 'rep', 0, 0, tiled=True, axis_index_groups=groups...  94.2 us
    all_to_all x1, blocking collectives, local(): sums = lax.all_to_all(partial, ('fsdp', 'tp'), 0, 0, tiled=True)  20.8 us
    pallas_call x1, Pallas kernels, encode(): pl.pallas_call(functools.partial(encode_kernel, where, spare, first, coun...  3.13 us

profile of v7, /device:TPU:1, one launch (start us, length us, event | category | flops | bytes accessed | tf_op | source)
XLA Modules:
  0.0 123.4 jit_solution(7490802232538996508)
XLA Ops:
  0.6 0.0 copy-start.10
  0.7 0.0 copy-start.11
  0.7 0.7 copy-done.10
  1.4 0.0 copy-done.11
  1.4 47.3 %conditional.1 = (s16[16,224,128]{2,1,0:T(8,128)(2,1)S(1)}) conditional(s32[]{:T(128)} %convert_element_type.3, (f32[1,16,1280]{2,1,0:T(8,128)}, bf16[1,16,1280]{2,1,0:T(8,128)(2,1)S(1)}, f32[1,16,6400]{2,1,0:T(8,128)}, bf16[1,16,6400]{2,1,0:T(8,128)(2,1)}, f32[1,16,6400]{2,1,0:T(8,128)}, /*index=5*/bf16[1,16,6400]{2,1,0:T(8,128)(2,1)}, ...), branch_computations={%region_0.1_spmd, %region_1.2_spmd} | conditional | bytes 3047520 | solution.py:236
  1.4 3.1 %encode.3 = s16[16,224,128]{2,1,0:T(8,128)(2,1)} custom-call(f32[1,16,1280]{2,1,0:T(8,128)} %get-tuple-element.37.refs_0_, bf16[1,16,1280]{2,1,0:T(8,128)(2,1)S(1)} %get-tuple-element.38.refs_1_, f32[1,16,6400]{2,1,0:T(8,128)} %get-tuple-element.39.refs_2_, bf16[1,16,6400]{2,1,0:T(8,128)(2,1)} %get-tuple-element.40.refs_3_, ...), custom_call_target="tpu_custom_call" | custom-call | tf_op jit(solution)/shard_map/cond/branch_0_fun/encode/pallas_call | solution.py:194
  4.6 42.7 %all_to_all.22.refs_0_ = s16[16,224,128]{2,1,0:T(8,128)(2,1)S(1)} all-to-all(s16[16,224,128]{2,1,0:T(8,128)(2,1)} %encode.3), channel_id=1, replica_groups={{320,288,256,224,192,160,128,96,64,32,0,480,448,416,384,352},{321,289,2..., dimensions={0} | all-to-all | bytes 1835008 | tf_op jit(solution)/shard_map/cond/branch_0_fun/all_to_all | solution.py:220
  47.3 1.4 %swap.2 = s16[16,224,128]{2,1,0:T(8,128)(2,1)S(1)} custom-call(s32[3,16]{1,0:T(4,128)S(1)} %get-tuple-element.23.partner_hbm, s32[1]{0:T(128)} %get-tuple-element.36.me, s16[16,224,128]{2,1,0:T(8,128)(2,1)S(1)} %all_to_all.22.refs_0_), custom_call_target="tpu_custom_call" | custom-call | tf_op jit(solution)/shard_map/cond/branch_0_fun/swap/pallas_call | solution.py:206
  48.7 0.0 copy-start.5
  48.8 0.0 copy-start.7
  48.8 0.0 copy-start.4
  48.8 51.5 %all_to_all.24.payload = s16[16,224,128]{2,1,0:T(8,128)(2,1)S(1)} all-to-all(s16[16,224,128]{2,1,0:T(8,128)(2,1)S(1)} %get-tuple-element.59), channel_id=1, replica_groups={{320,288,256,224,192,160,128,96,64,32,0,480,448,416,384,352},{321,289,2..., dimensions={0} | all-to-all | bytes 1835008 | tf_op jit(solution)/shard_map/all_to_all | solution.py:220
  100.3 0.0 copy-done.5
  100.3 0.0 copy-done.7
  100.3 0.0 copy-start
  100.3 0.0 copy-start.1
  100.3 0.0 copy-start.2
  100.3 0.0 copy-start.3
  100.3 0.0 copy-start.8
  100.3 0.5 squares.1
  100.8 20.8 %all_to_all.25.sums = f32[32,1,128]{2,1,0:T(1,128)S(1)} all-to-all(f32[32,1,128]{2,1,0:T(1,128)S(1)} %squares.1), channel_id=1, replica_groups=mesh['rep'=16,'fsdp'=8,'tp'=4] {'fsdp','tp'}, dimensions={0} | all-to-all | bytes 32768 | tf_op jit(solution)/shard_map/all_to_all | solution.py:251
  121.6 0.0 copy-done.4
  121.6 0.0 copy-done
  121.6 0.0 copy-done.1
  121.6 0.0 copy-done.2
  121.6 0.0 copy-done.3
  121.6 0.0 copy-done.8
  121.7 1.8 %update.1 = (f32[1,16,6400]{2,1,0:T(8,128)}, f32[1,16,6400]{2,1,0:T(8,128)}, f32[1,16,1280]{2,1,0:T(8,128)}, f32[1,16,6400]{2,1,0:T(8,128)}, f32[1,16,6400]{2,1,0:T(8,128)}, /*index=5*/f32[1,16,1280]{2,1,0:T(8,128)}) custom-call(f32[32,1,128]{2,1,0:T(1,128)S(1)} %all_to_all.25.sums, s16[16,224,128]{2,1,0:T(8,128)(2,1)S(1)} %all_to_all.24.payload, ...), custom_call_target="tpu_custom_call" | custom-call | tf_op jit(solution)/shard_map/update/pallas_call | solution.py:254
Async XLA Ops:
  0.6 0.8 copy-start.10
  0.7 0.7 copy-start.11
  48.7 51.5 %copy-start.5 = (bf16[1,16,6400]{2,1,0:T(8,128)(2,1)S(1)}, bf16[1,16,6400]{2,1,0:T(8,128)(2,1)}, u32[]{:S(2)}) copy-start(bf16[1,16,6400]{2,1,0:T(8,128)(2,1)} %gg.3) | copy-start | bytes 614404
  48.8 51.5 %copy-start.7 = (bf16[1,16,6400]{2,1,0:T(8,128)(2,1)S(1)}, bf16[1,16,6400]{2,1,0:T(8,128)(2,1)}, u32[]{:S(2)}) copy-start(bf16[1,16,6400]{2,1,0:T(8,128)(2,1)} %gu.3) | copy-start | bytes 614404
  48.8 72.8 %copy-start.4 = (f32[1,16,6400]{2,1,0:T(8,128)S(1)}, f32[1,16,6400]{2,1,0:T(8,128)}, u32[]{:S(2)}) copy-start(f32[1,16,6400]{2,1,0:T(8,128)} %wu.1) | copy-start | bytes 1228804
  100.3 21.3 %copy-start = (f32[1,16,6400]{2,1,0:T(8,128)S(1)}, f32[1,16,6400]{2,1,0:T(8,128)}, u32[]{:S(2)}) copy-start(f32[1,16,6400]{2,1,0:T(8,128)} %mg.1) | copy-start | bytes 1228804
  100.3 21.3 %copy-start.1 = (f32[1,16,6400]{2,1,0:T(8,128)S(1)}, f32[1,16,6400]{2,1,0:T(8,128)}, u32[]{:S(2)}) copy-start(f32[1,16,6400]{2,1,0:T(8,128)} %mu.1) | copy-start | bytes 1228804
  100.3 21.3 %copy-start.2 = (f32[1,16,1280]{2,1,0:T(8,128)S(1)}, f32[1,16,1280]{2,1,0:T(8,128)}, u32[]{:S(2)}) copy-start(f32[1,16,1280]{2,1,0:T(8,128)} %md.1) | copy-start | bytes 245764
  100.3 21.3 %copy-start.3 = (f32[1,16,6400]{2,1,0:T(8,128)S(1)}, f32[1,16,6400]{2,1,0:T(8,128)}, u32[]{:S(2)}) copy-start(f32[1,16,6400]{2,1,0:T(8,128)} %wg.1) | copy-start | bytes 1228804
  100.3 21.3 %copy-start.8 = (f32[1,16,1280]{2,1,0:T(8,128)S(1)}, f32[1,16,1280]{2,1,0:T(8,128)}, u32[]{:S(2)}) copy-start(f32[1,16,1280]{2,1,0:T(8,128)} %wd.1) | copy-start | bytes 245764

commit v8 on v7

--- a/solution.py
+++ b/solution.py
@@ -18,7 +18,7 @@
 STEPS = 16.0
 TINY = 2.0**-120
 REPLICAS = 16
-ORDER = 10
+ORDER = 12
 VMEM_LIMIT = 24 * 1024 * 1024
 ENCODE_LIMIT = 60 * 1024 * 1024
 

time: 124 us -> 131 us (1.056)
  blocking collectives: 115 us -> 122 us
    all_to_all x2, blocking collectives: 94.2 us -> 98.6 us  [send(): lax.all_to_all(payload, 'rep', 0, 0, tiled=True, axis_index_groups=groups...]
    all_to_all x1, blocking collectives: 20.8 us -> 23.2 us  [local(): sums = lax.all_to_all(partial, ('fsdp', 'tp'), 0, 0, tiled=True)]
where the time goes in v8:
time: 131 us; the launch traced here: 130 us
  blocking collectives  122 us (93%)
  Pallas kernels  6.78 us (5%)
    all_to_all x2, blocking collectives, send(): lax.all_to_all(payload, 'rep', 0, 0, tiled=True, axis_index_groups=groups...  98.6 us
    all_to_all x1, blocking collectives, local(): sums = lax.all_to_all(partial, ('fsdp', 'tp'), 0, 0, tiled=True)  23.2 us
    pallas_call x1, Pallas kernels, encode(): pl.pallas_call(functools.partial(encode_kernel, where, spare, first, coun...  3.13 us

profile of v8, /device:TPU:1, one launch (start us, length us, event | category | flops | bytes accessed | tf_op | source)
XLA Modules:
  0.0 130.1 jit_solution(14479397594427413427)
XLA Ops:
  0.6 0.0 copy-start.10
  0.7 0.0 copy-start.11
  0.7 0.7 copy-done.10
  1.4 0.0 copy-done.11
  1.4 42.3 %conditional.1 = (s16[16,224,128]{2,1,0:T(8,128)(2,1)S(1)}) conditional(s32[]{:T(128)} %convert_element_type.3, (f32[1,16,1280]{2,1,0:T(8,128)}, bf16[1,16,1280]{2,1,0:T(8,128)(2,1)S(1)}, f32[1,16,6400]{2,1,0:T(8,128)}, bf16[1,16,6400]{2,1,0:T(8,128)(2,1)}, f32[1,16,6400]{2,1,0:T(8,128)}, /*index=5*/bf16[1,16,6400]{2,1,0:T(8,128)(2,1)}, ...), branch_computations={%region_0.1_spmd, %region_1.2_spmd} | conditional | bytes 3047520 | solution.py:236
  1.4 3.1 %encode.3 = s16[16,224,128]{2,1,0:T(8,128)(2,1)} custom-call(f32[1,16,1280]{2,1,0:T(8,128)} %get-tuple-element.37.refs_0_, bf16[1,16,1280]{2,1,0:T(8,128)(2,1)S(1)} %get-tuple-element.38.refs_1_, f32[1,16,6400]{2,1,0:T(8,128)} %get-tuple-element.39.refs_2_, bf16[1,16,6400]{2,1,0:T(8,128)(2,1)} %get-tuple-element.40.refs_3_, ...), custom_call_target="tpu_custom_call" | custom-call | tf_op jit(solution)/shard_map/cond/branch_0_fun/encode/pallas_call | solution.py:194
  4.6 37.7 %all_to_all.22.refs_0_ = s16[16,224,128]{2,1,0:T(8,128)(2,1)S(1)} all-to-all(s16[16,224,128]{2,1,0:T(8,128)(2,1)} %encode.3), channel_id=1, replica_groups={{384,352,320,288,256,224,192,160,128,96,64,32,0,480,448,416},{385,353,3..., dimensions={0} | all-to-all | bytes 1835008 | tf_op jit(solution)/shard_map/cond/branch_0_fun/all_to_all | solution.py:220
  42.3 1.4 %swap.2 = s16[16,224,128]{2,1,0:T(8,128)(2,1)S(1)} custom-call(s32[3,16]{1,0:T(4,128)S(1)} %get-tuple-element.23.partner_hbm, s32[1]{0:T(128)} %get-tuple-element.36.me, s16[16,224,128]{2,1,0:T(8,128)(2,1)S(1)} %all_to_all.22.refs_0_), custom_call_target="tpu_custom_call" | custom-call | tf_op jit(solution)/shard_map/cond/branch_0_fun/swap/pallas_call | solution.py:206
  43.7 0.0 copy-start.5
  43.8 0.0 copy-start.7
  43.8 0.0 copy-start.4
  43.8 60.8 %all_to_all.24.payload = s16[16,224,128]{2,1,0:T(8,128)(2,1)S(1)} all-to-all(s16[16,224,128]{2,1,0:T(8,128)(2,1)S(1)} %get-tuple-element.59), channel_id=1, replica_groups={{384,352,320,288,256,224,192,160,128,96,64,32,0,480,448,416},{385,353,3..., dimensions={0} | all-to-all | bytes 1835008 | tf_op jit(solution)/shard_map/all_to_all | solution.py:220
  104.6 0.0 copy-done.5
  104.6 0.0 copy-done.7
  104.6 0.0 copy-start
  104.6 0.0 copy-start.1
  104.6 0.0 copy-start.2
  104.6 0.0 copy-start.3
  104.7 0.0 copy-start.8
  104.7 0.5 squares.1
  105.1 23.2 %all_to_all.25.sums = f32[32,1,128]{2,1,0:T(1,128)S(1)} all-to-all(f32[32,1,128]{2,1,0:T(1,128)S(1)} %squares.1), channel_id=1, replica_groups=mesh['rep'=16,'fsdp'=8,'tp'=4] {'fsdp','tp'}, dimensions={0} | all-to-all | bytes 32768 | tf_op jit(solution)/shard_map/all_to_all | solution.py:251
  128.3 0.0 copy-done.4
  128.3 0.0 copy-done
  128.3 0.0 copy-done.1
  128.3 0.0 copy-done.2
  128.3 0.0 copy-done.3
  128.4 0.0 copy-done.8
  128.4 1.8 %update.1 = (f32[1,16,6400]{2,1,0:T(8,128)}, f32[1,16,6400]{2,1,0:T(8,128)}, f32[1,16,1280]{2,1,0:T(8,128)}, f32[1,16,6400]{2,1,0:T(8,128)}, f32[1,16,6400]{2,1,0:T(8,128)}, /*index=5*/f32[1,16,1280]{2,1,0:T(8,128)}) custom-call(f32[32,1,128]{2,1,0:T(1,128)S(1)} %all_to_all.25.sums, s16[16,224,128]{2,1,0:T(8,128)(2,1)S(1)} %all_to_all.24.payload, ...), custom_call_target="tpu_custom_call" | custom-call | tf_op jit(solution)/shard_map/update/pallas_call | solution.py:254
Async XLA Ops:
  0.6 0.8 copy-start.10
  0.7 0.7 copy-start.11
  43.7 60.9 %copy-start.5 = (bf16[1,16,6400]{2,1,0:T(8,128)(2,1)S(1)}, bf16[1,16,6400]{2,1,0:T(8,128)(2,1)}, u32[]{:S(2)}) copy-start(bf16[1,16,6400]{2,1,0:T(8,128)(2,1)} %gg.3) | copy-start | bytes 614404
  43.8 60.9 %copy-start.7 = (bf16[1,16,6400]{2,1,0:T(8,128)(2,1)S(1)}, bf16[1,16,6400]{2,1,0:T(8,128)(2,1)}, u32[]{:S(2)}) copy-start(bf16[1,16,6400]{2,1,0:T(8,128)(2,1)} %gu.3) | copy-start | bytes 614404
  43.8 84.6 %copy-start.4 = (f32[1,16,6400]{2,1,0:T(8,128)S(1)}, f32[1,16,6400]{2,1,0:T(8,128)}, u32[]{:S(2)}) copy-start(f32[1,16,6400]{2,1,0:T(8,128)} %wu.1) | copy-start | bytes 1228804
  104.6 23.7 %copy-start = (f32[1,16,6400]{2,1,0:T(8,128)S(1)}, f32[1,16,6400]{2,1,0:T(8,128)}, u32[]{:S(2)}) copy-start(f32[1,16,6400]{2,1,0:T(8,128)} %mg.1) | copy-start | bytes 1228804
  104.6 23.7 %copy-start.1 = (f32[1,16,6400]{2,1,0:T(8,128)S(1)}, f32[1,16,6400]{2,1,0:T(8,128)}, u32[]{:S(2)}) copy-start(f32[1,16,6400]{2,1,0:T(8,128)} %mu.1) | copy-start | bytes 1228804
  104.6 23.7 %copy-start.2 = (f32[1,16,1280]{2,1,0:T(8,128)S(1)}, f32[1,16,1280]{2,1,0:T(8,128)}, u32[]{:S(2)}) copy-start(f32[1,16,1280]{2,1,0:T(8,128)} %md.1) | copy-start | bytes 245764
  104.6 23.7 %copy-start.3 = (f32[1,16,6400]{2,1,0:T(8,128)S(1)}, f32[1,16,6400]{2,1,0:T(8,128)}, u32[]{:S(2)}) copy-start(f32[1,16,6400]{2,1,0:T(8,128)} %wg.1) | copy-start | bytes 1228804
  104.7 23.7 %copy-start.8 = (f32[1,16,1280]{2,1,0:T(8,128)S(1)}, f32[1,16,1280]{2,1,0:T(8,128)}, u32[]{:S(2)}) copy-start(f32[1,16,1280]{2,1,0:T(8,128)} %wd.1) | copy-start | bytes 245764
